TPU v7x, 256 devices: a whole 4x4x8 slice. The times are simulated.
256 devices in a mesh: seq: 16 (over z_hi, x), ch: 16 (over z_lo, y, core).
Axes of the slice: x: 4, y: 4, z: 8 (z_hi: 4, z_lo: 2; z = z_hi * 2 + z_lo), core: 2. Of those that a mesh axis runs over, the one named last changes fastest.
Arguments:
- strands: bfloat16 [2, 32768, 512], P(None, ('seq', 'ch')), may hold values from -24 to 24
- cotangent: bfloat16 [2, 32768, 512], P(None, ('seq', 'ch')), may hold values from -6 to 6
- proj_in: bfloat16 [512, 3072], P('ch'), may hold values from -0.25 to 0.25
- proj_out: bfloat16 [1024, 512], P('ch'), may hold values from -0.1875 to 0.1875
- short_taps: float32 [3072, 4], replicated, may hold values from -3 to 3
- filters: bfloat16 [64, 128], replicated, may hold values from -0.5 to 0.5
Outputs:
- strands_out: bfloat16 [2, 32768, 512], P(None, ('seq', 'ch'))
- grad_strands: bfloat16 [2, 32768, 512], P(None, ('seq', 'ch'))
- grad_proj_in: float32 [512, 3072], P('ch')
- grad_proj_out: float32 [1024, 512], P('ch')
- grad_short: float32 [3072, 4], P('ch')
- grad_filters: float32 [64, 128], P('ch')
All inputs are finite; a program needn't handle non-finite values.
Results may differ from a plain program's by a relative error of at most 0.017.
Values may be sent and summed in bfloat16 or wider, within the bound.
A program may use at most 128 MiB of HBM per device.

v0:
```python
import jax
import jax.numpy as jnp
from jax import lax
from jax.sharding import PartitionSpec as P


def swapped(shard, axis, distance):
    return lax.ppermute(shard, axis, [(i, i ^ 1 << distance) for i in range(lax.axis_size(axis))])


def from_behind(block, axis, distance):
    devices = range(lax.axis_size(axis))
    route = [(i - distance, i) for i in devices if i - distance in devices]
    return lax.ppermute(block, axis, route)


def flipped(segment):
    return segment[::-1, ::-1]


def mirrored(segment):
    levels = lax.axis_size(("seq", "ch")).bit_length() - 1
    for bit_index in range(levels):
        segment = swapped(segment, ("seq", "ch"), bit_index)
    return segment


def edge_rows(pieces, leading):
    moved = from_behind(pieces, ("seq", "ch"), 1 if leading else -1)
    return moved


def toeplitz_table(filters):
    group_count = filters.shape[0]
    filter_tap_count = filters.shape[1]
    head_zero = jnp.zeros((group_count, 1), filters.dtype)
    tail_zero = jnp.zeros((group_count, 2 * filter_tap_count - 1), filters.dtype)
    pattern = jnp.concatenate([head_zero, filters[:, ::-1], tail_zero], axis=1)
    repeated = jnp.tile(pattern, (1, filter_tap_count))
    skewed = repeated[:, : filter_tap_count * (3 * filter_tap_count - 1)].reshape(
        group_count, filter_tap_count, 3 * filter_tap_count - 1
    )
    return skewed[:, :, : 2 * filter_tap_count]


def windows_of(extended, filter_tap_count, group_size):
    strand_count = extended.shape[0]
    ext_rows = extended.shape[1]
    channels = extended.shape[2]
    pieces = extended.reshape(
        strand_count,
        ext_rows // filter_tap_count,
        filter_tap_count,
        channels // group_size,
        group_size,
    )
    return jnp.concatenate([pieces[:, :-1], pieces[:, 1:]], axis=2)


def long_conv(extended, toeplitz, group_size):
    windows = windows_of(extended, toeplitz.shape[1], group_size)
    output = jnp.einsum("gij,sbjgc->sbigc", toeplitz, windows, preferred_element_type=jnp.float32)
    return output.reshape(extended.shape[0], -1, extended.shape[2])


def unskew(products):
    group_count = products.shape[0]
    filter_tap_count = products.shape[1]
    padded = jnp.pad(products, ((0, 0), (0, 0), (0, filter_tap_count - 1)))
    flattened = padded.reshape(group_count, filter_tap_count * (3 * filter_tap_count - 1))
    flattened = jnp.pad(flattened, ((0, 0), (0, filter_tap_count)))
    sheared = flattened.reshape(group_count, filter_tap_count, 3 * filter_tap_count)
    summed = jnp.sum(sheared, axis=1)
    return summed[:, 1 : filter_tap_count + 1][:, ::-1]


def filter_grad(extended, grad_conv, group_size, filter_tap_count):
    windows = windows_of(extended, filter_tap_count, group_size)
    grad_pieces = grad_conv.reshape(
        windows.shape[0], windows.shape[1], filter_tap_count, windows.shape[3], group_size
    )
    products = jnp.einsum(
        "sbigc,sbjgc->gij", grad_pieces, windows, preferred_element_type=jnp.float32
    )
    return unskew(products)


def reduce_terms(terms):
    shares = (
        lax.psum_scatter(terms[0], "ch", scatter_dimension=0, tiled=True),
        lax.psum_scatter(terms[1], "ch", scatter_dimension=0, tiled=True),
        lax.psum_scatter(terms[2], "ch", scatter_dimension=0, tiled=True),
        lax.psum_scatter(terms[3], "ch", scatter_dimension=0, tiled=True),
    )
    return lax.psum((shares[0], shares[1], shares[2], shares[3]), "seq")


def shards(strands, cotangent, proj_in, proj_out, short_taps, filters):
    complete_input, whole_out = (
        lax.all_gather(proj_in, "ch", axis=0, tiled=True),
        lax.all_gather(proj_out, "ch", axis=0, tiled=True),
    )
    tok_count = strands.shape[1]
    short_len = short_taps.shape[1]
    filter_tap_count = filters.shape[1]
    channels = whole_out.shape[0]
    group_size = channels // filters.shape[0]
    second_in = flipped(mirrored(strands[1]))
    second_cot = flipped(mirrored(cotangent[1]))
    input_batch = jnp.stack([strands[0], second_in])
    cotangents = jnp.stack([cotangent[0], second_cot])
    projected = jnp.einsum(
        "rax,xt->rat", input_batch, complete_input, preferred_element_type=jnp.float32
    ).astype(jnp.bfloat16)
    before_proj = edge_rows(projected[:, tok_count - (short_len - 1) :], True)
    proj_ext = jnp.concatenate([before_proj, projected], axis=1)
    mixer_output = jnp.zeros(projected.shape, jnp.float32)
    for shift_at in range(short_len):
        start_row = short_len - 1 - shift_at
        mixer_output = mixer_output + short_taps[:, shift_at] * proj_ext[
            :, start_row : start_row + tok_count
        ].astype(jnp.float32)
    query_part = mixer_output[:, :, :channels]
    key_part = mixer_output[:, :, channels : 2 * channels]
    value_part = mixer_output[:, :, 2 * channels :]
    gated_prod = (key_part * value_part).astype(jnp.bfloat16)
    before_gated = edge_rows(gated_prod[:, tok_count - (filter_tap_count - 1) :], True)
    zero_row = jnp.zeros((2, 1, channels), jnp.bfloat16)
    gated_ext = jnp.concatenate([zero_row, before_gated, gated_prod], axis=1)
    toeplitz = toeplitz_table(filters)
    conv_out = long_conv(gated_ext, toeplitz, group_size)
    hidden = (query_part * conv_out).astype(jnp.bfloat16)
    produced = jnp.einsum(
        "sle,eh->slh", hidden, whole_out, preferred_element_type=jnp.float32
    ).astype(jnp.bfloat16)
    grad_hidden = jnp.einsum(
        "slh,eh->sle", cotangents, whole_out, preferred_element_type=jnp.float32
    ).astype(jnp.bfloat16)
    part_out = jnp.einsum("sle,slh->eh", hidden, cotangents, preferred_element_type=jnp.float32)
    hidden_grad = grad_hidden.astype(jnp.float32)
    query_gradient = hidden_grad * conv_out
    grad_conv = (hidden_grad * query_part).astype(jnp.bfloat16)
    after_conv = edge_rows(grad_conv[:, : filter_tap_count - 1], False)
    grad_ext = jnp.concatenate([zero_row, after_conv[:, ::-1], grad_conv[:, ::-1]], axis=1)
    grad_gated = long_conv(grad_ext, toeplitz, group_size)[:, ::-1]
    part_filters = filter_grad(gated_ext, grad_conv, group_size, filter_tap_count)
    grad_mixed = jnp.concatenate(
        [query_gradient, grad_gated * value_part, grad_gated * key_part], axis=2
    ).astype(jnp.bfloat16)
    after_mixed = edge_rows(grad_mixed[:, : short_len - 1], False)
    mixed_ext = jnp.concatenate([grad_mixed, after_mixed], axis=1)
    grad_sum = jnp.zeros(grad_mixed.shape, jnp.float32)
    for shift_at in range(short_len):
        grad_sum = grad_sum + short_taps[:, shift_at] * mixed_ext[
            :, shift_at : shift_at + tok_count
        ].astype(jnp.float32)
    projection_gradient = grad_sum.astype(jnp.bfloat16)
    mixed_grad = grad_mixed.astype(jnp.float32)
    columns = []
    for shift_at in range(short_len):
        start_row = short_len - 1 - shift_at
        columns.append(
            jnp.sum(
                proj_ext[:, start_row : start_row + tok_count].astype(jnp.float32) * mixed_grad,
                axis=(0, 1),
            )
        )
    part_short = jnp.stack(columns, axis=1)
    grad_inputs = jnp.einsum(
        "qij,ej->qie", projection_gradient, complete_input, preferred_element_type=jnp.float32
    ).astype(jnp.bfloat16)
    partial_input = jnp.einsum(
        "wea,wem->am", input_batch, projection_gradient, preferred_element_type=jnp.float32
    )
    out_second = mirrored(flipped(produced[1]))
    grad_second = mirrored(flipped(grad_inputs[1]))
    strands_out = jnp.stack([produced[0], out_second])
    grad_strands = jnp.stack([grad_inputs[0], grad_second])
    totals = reduce_terms((partial_input, part_out, part_short, part_filters))
    grad_scale = float(tok_count * lax.axis_size(("seq", "ch"))) ** (-0.5)
    return (
        strands_out,
        grad_strands,
        totals[0] * grad_scale,
        totals[1] * grad_scale,
        totals[2] * grad_scale,
        totals[3] * grad_scale,
    )


def solution(mesh):
    placed = (
        P(None, ("seq", "ch"), None),
        P(None, ("seq", "ch"), None),
        P("ch", None),
        P("ch", None),
        P(),
        P(),
    )
    return jax.shard_map(
        shards,
        mesh=mesh,
        in_specs=placed,
        out_specs=(
            P(None, ("seq", "ch"), None),
            P(None, ("seq", "ch"), None),
            P("ch", None),
            P("ch", None),
            P("ch", None),
            P("ch", None),
        ),
        check_vma=False,
    )
```

profile of v0, /device:TPU:8, one launch (start us, length us, event | category | flops | bytes accessed | tf_op | source)
XLA Modules:
  0.0 596.5 jit_solution(14838568816899748740)
XLA Ops:
  14.4 3.3 collective-permute-done.1
  21.9 3.0 collective-permute-done.2
  34.1 3.8 collective-permute-done.4
  44.3 3.1 collective-permute-start.6
  52.8 9.8 %collective-permute-start.7 = (bf16[128,512]{1,0:T(8,128)(2,1)S(1)}, bf16[128,512]{1,0:T(8,128)(2,1)S(1)}, u32[]{:S(2)}, u32[]{:S(2)}) collective-permute-start(bf16[128,512]{1,0:T(8,128)(2,1)S(1)} %collective-permute-done.6), channel_id=1, source_target_pairs={{0,128},{1,129},{2,130},{3,131},{4,132},{5,133},{6,134},{7,135},{8... | collective-permute-start | bytes 393224 | tf_op jit(solution)/shard_map/ppermute | solution.py:8
  76.3 4.8 fusion.4
  81.0 12.0 %all-gather.5.cloned.1.call-done = bf16[1024,512]{1,0:T(8,128)(2,1)} async-done(((bf16[64,512]{1,0:T(8,128)(2,1)}), bf16[1024,512]{1,0:T(8,128)(2,1)}) %all-gather.5.cloned.1.call-update) | async-done | bytes 1048592 | tf_op jit(solution)/shard_map/all_gather | solution.py:101
  101.5 4.1 copy.60
  105.6 3.1 slice.148
  108.7 16.5 %reshape.58 = bf16[64,128,383]{2,1,0:T(8,128)(2,1)} reshape(bf16[64,49024]{1,0:T(8,128)(2,1)} %slice.148) | data formatting | bytes 12550144 | tf_op jit(solution)/shard_map/reshape | solution.py:40
  125.2 8.3 %rev.32 = bf16[2,128,1024]{2,1,0:T(8,128)(2,1)} reverse(bf16[2,128,1024]{2,1,0:T(8,128)(2,1)} %get-tuple-element.35), dimensions={1} | reverse | bytes 1048576 | tf_op jit(solution)/shard_map/rev | solution.py:144
  133.5 8.4 %rev.31 = bf16[2,127,1024]{2,1,0:T(8,128)(2,1)} reverse(bf16[2,127,1024]{2,1,0:T(8,128)(2,1)} %collective-permute-done.26), dimensions={1} | reverse | bytes 1040384 | tf_op jit(solution)/shard_map/rev | solution.py:144
  148.9 3.4 fusion.35
  157.7 8.9 %rev.33 = f32[2,128,1024]{2,1,0:T(8,128)} reverse(f32[2,128,1024]{2,1,0:T(8,128)} %copy.46), dimensions={1} | reverse | bytes 2097152 | tf_op jit(solution)/shard_map/rev | solution.py:145
  171.9 7.9 %collective-permute-done.9 = bf16[2,127,1024]{2,1,0:T(8,128)(2,1)S(1)} collective-permute-done((bf16[2,127,1024]{2,1,0:T(8,128)(2,1)S(1)}, bf16[2,127,1024]{2,1,0:T(8,128)(2,1)S(1)}, u32[]{:S(2)}, u32[]{:S(2)}) %collective-permute-start.9) | collective-permute-done | bytes 520224 | tf_op jit(solution)/shard_map/ppermute | solution.py:14
  185.7 3.4 fusion.36
  189.3 4.0 fusion.18
  211.6 3.7 convolution_bitcast_fusion
  225.2 4.9 collective-permute-done.11
  230.1 6.1 %collective-permute-start.12 = (bf16[128,512]{1,0:T(8,128)(2,1)S(1)}, bf16[128,512]{1,0:T(8,128)(2,1)S(1)}, u32[]{:S(2)}, u32[]{:S(2)}) collective-permute-start(bf16[128,512]{1,0:T(8,128)(2,1)S(1)} %collective-permute-done.11), channel_id=1, source_target_pairs={{0,4},{1,5},{2,6},{3,7},{4,0},{5,1},{6,2},{7,3},{8,12},{9,13},{10,... | collective-permute-start | bytes 393224 | tf_op jit(solution)/shard_map/ppermute | solution.py:8
  236.2 3.5 collective-permute-start.30
  248.2 6.3 %pad.8 = f32[64,128,383]{2,1,0:T(8,128)} pad(f32[64,128,256]{2,1,0:T(8,128)S(1)} %convolution_bitcast_fusion.1, f32[]{:T(128)} %constant.5.clone.1), padding=0_0x0_0x0_127 | pad | bytes 20938756 | tf_op jit(solution)/shard_map/jit(_pad)/pad | solution.py:69
  254.5 14.1 %reshape.64 = f32[64,49024]{1,0:T(8,128)} reshape(f32[64,128,383]{2,1,0:T(8,128)} %pad.8) | data formatting | bytes 25100288 | tf_op jit(solution)/shard_map/reshape | solution.py:70
  268.6 10.2 %pad.9 = f32[64,49152]{1,0:T(8,128)} pad(f32[64,49024]{1,0:T(8,128)} %reshape.64, f32[]{:T(128)} %constant.5.clone.1), padding=0_0x0_128 | pad | bytes 25133060 | tf_op jit(solution)/shard_map/jit(_pad)/pad | solution.py:71
  278.7 11.4 %copy.61 = f32[8,8,128,384]{3,2,1,0:T(8,128)} copy(f32[8,8,128,384]{3,1,2,0:T(8,128)} %bitcast.88) | data formatting | bytes 25165824
  292.1 6.0 %bitcast_reduce_fusion = f32[64,384]{1,0:T(8,128)S(1)} fusion(f32[8,8,128,384]{3,2,1,0:T(8,128)} %copy.61), kind=kLoop, calls=%fused_computation | loop fusion | flops 3121152 | bytes 12681216 | tf_op jit(solution)/shard_map/reduce_sum | solution.py:73
  301.9 51.1 %all-reduce.2 = f32[64,128]{1,0:T(8,128)S(1)} all-reduce(f32[64,128]{1,0:T(8,128)S(1)} %rev.35), channel_id=5, replica_groups=mesh['seq'=16,'ch'=16] {'ch'}, use_global_device_ids=true, to_apply=%region_11.12.clone | all-reduce | flops 8192 | bytes 65536
  354.0 43.9 %all-reduce.3 = (f32[192,4]{0,1:T(4,128)S(1)}, f32[4,128]{1,0:T(4,128)S(1)}) all-reduce(f32[192,4]{0,1:T(4,128)S(1)} %copy.55, f32[4,128]{1,0:T(4,128)S(1)} %constant_dynamic-slice_fusion), channel_id=1, replica_groups=mesh['seq'=16,'ch'=16] {'seq'}, use_global_device_ids=true, to_apply=%region_9.10 | all-reduce | flops 1280 | bytes 10240 | tf_op jit(solution)/shard_map/psum | solution.py:95
  400.9 11.4 %reduce-scatter.6.cloned.1.call-done = f32[32,3072]{1,0:T(8,128)} async-done(((f32[512,3072]{1,0:T(8,128)}), f32[32,3072]{1,0:T(8,128)}) %reduce-scatter.6.cloned.1.call-update) | async-done | bytes 393232 | tf_op jit(solution)/shard_map/reduce_scatter | solution.py:90
  413.0 5.1 collective-permute-start.17
  419.5 4.9 collective-permute-done.17
  428.2 157.8 %all-reduce.7.cloned.1.call-done = (f32[32,3072]{1,0:T(8,128)}, f32[64,512]{1,0:T(8,128)}) async-done(((f32[32,3072]{1,0:T(8,128)}, f32[64,512]{1,0:T(8,128)}), (f32[32,3072]{1,0:T(8,128)}, f32[64,512]{1,0:T(8,128)})) %all-reduce.7.cloned.1.call-update) | async-done | bytes 524304 | tf_op jit(solution)/shard_map/psum | solution.py:95
  (186 shorter events, 132.9 us)
Async XLA Ops:
  7.2 59.0 %all-gather.3.cloned.1.call-start = ((), (), s32[]{:S(2)}) async-start(), calls=%async_computation.3 | async-start | bytes 3342336 | tf_op jit(solution)/shard_map/all_gather | solution.py:100
  7.9 85.2 %all-gather.5.cloned.1.call-start = ((), (), s32[]{:S(2)}) async-start(), calls=%async_computation.4 | async-start | bytes 1114112 | tf_op jit(solution)/shard_map/all_gather | solution.py:101
  13.4 6.6 %collective-permute-start.19 = (bf16[128,512]{1,0:T(8,128)(2,1)S(1)}, bf16[128,512]{1,0:T(8,128)(2,1)S(1)}, u32[]{:S(2)}, u32[]{:S(2)}) collective-permute-start(bf16[128,512]{1,0:T(8,128)(2,1)S(1)} %collective-permute-done.18), channel_id=1, source_target_pairs={{0,2},{1,3},{2,0},{3,1},{4,6},{5,7},{6,4},{7,5},{8,10},{9,11},{10,... | collective-permute-start | bytes 393224 | tf_op jit(solution)/shard_map/ppermute | solution.py:8
  17.7 7.2 %collective-permute-start.2 = (bf16[128,512]{1,0:T(8,128)(2,1)S(1)}, bf16[128,512]{1,0:T(8,128)(2,1)S(1)}, u32[]{:S(2)}, u32[]{:S(2)}) collective-permute-start(bf16[128,512]{1,0:T(8,128)(2,1)S(1)} %collective-permute-done.1), channel_id=1, source_target_pairs={{0,4},{1,5},{2,6},{3,7},{4,0},{5,1},{6,2},{7,3},{8,12},{9,13},{10,... | collective-permute-start | bytes 393224 | tf_op jit(solution)/shard_map/ppermute | solution.py:8
  20.0 7.3 %collective-permute-start.20 = (bf16[128,512]{1,0:T(8,128)(2,1)S(1)}, bf16[128,512]{1,0:T(8,128)(2,1)S(1)}, u32[]{:S(2)}, u32[]{:S(2)}) collective-permute-start(bf16[128,512]{1,0:T(8,128)(2,1)S(1)} %collective-permute-done.19), channel_id=1, source_target_pairs={{0,4},{1,5},{2,6},{3,7},{4,0},{5,1},{6,2},{7,3},{8,12},{9,13},{10,... | collective-permute-start | bytes 393224 | tf_op jit(solution)/shard_map/ppermute | solution.py:8
  24.9 6.6 %collective-permute-start.3 = (bf16[128,512]{1,0:T(8,128)(2,1)S(1)}, bf16[128,512]{1,0:T(8,128)(2,1)S(1)}, u32[]{:S(2)}, u32[]{:S(2)}) collective-permute-start(bf16[128,512]{1,0:T(8,128)(2,1)S(1)} %collective-permute-done.2), channel_id=1, source_target_pairs={{0,8},{1,9},{2,10},{3,11},{4,12},{5,13},{6,14},{7,15},{8,0},{9,1},... | collective-permute-start | bytes 393224 | tf_op jit(solution)/shard_map/ppermute | solution.py:8
  32.9 7.7 %collective-permute-start.22 = (bf16[128,512]{1,0:T(8,128)(2,1)S(1)}, bf16[128,512]{1,0:T(8,128)(2,1)S(1)}, u32[]{:S(2)}, u32[]{:S(2)}) collective-permute-start(bf16[128,512]{1,0:T(8,128)(2,1)S(1)} %collective-permute-done.21), channel_id=1, source_target_pairs={{0,16},{1,17},{2,18},{3,19},{4,20},{5,21},{6,22},{7,23},{8,24},{9,... | collective-permute-start | bytes 393224 | tf_op jit(solution)/shard_map/ppermute | solution.py:8
  40.6 6.9 %collective-permute-start.23 = (bf16[128,512]{1,0:T(8,128)(2,1)S(1)}, bf16[128,512]{1,0:T(8,128)(2,1)S(1)}, u32[]{:S(2)}, u32[]{:S(2)}) collective-permute-start(bf16[128,512]{1,0:T(8,128)(2,1)S(1)} %collective-permute-done.22), channel_id=1, source_target_pairs={{0,32},{1,33},{2,34},{3,35},{4,36},{5,37},{6,38},{7,39},{8,40},{9,... | collective-permute-start | bytes 393224 | tf_op jit(solution)/shard_map/ppermute | solution.py:8
  44.3 8.4 %collective-permute-start.6 = (bf16[128,512]{1,0:T(8,128)(2,1)S(1)}, bf16[128,512]{1,0:T(8,128)(2,1)S(1)}, u32[]{:S(2)}, u32[]{:S(2)}) collective-permute-start(bf16[128,512]{1,0:T(8,128)(2,1)S(1)} %collective-permute-done.5), channel_id=1, source_target_pairs={{0,64},{1,65},{2,66},{3,67},{4,68},{5,69},{6,70},{7,71},{8,72},{9,... | collective-permute-start | bytes 393224 | tf_op jit(solution)/shard_map/ppermute | solution.py:8
  47.4 305.6 %reduce-scatter.10.cloned.1.call-start = ((), (), s32[]{:S(2)}) async-start(), calls=%async_computation.7 | async-start | bytes 1671168
  47.5 15.0 %collective-permute-start.24 = (bf16[128,512]{1,0:T(8,128)(2,1)S(1)}, bf16[128,512]{1,0:T(8,128)(2,1)S(1)}, u32[]{:S(2)}, u32[]{:S(2)}) collective-permute-start(bf16[128,512]{1,0:T(8,128)(2,1)S(1)} %collective-permute-done.23), channel_id=1, source_target_pairs={{0,64},{1,65},{2,66},{3,67},{4,68},{5,69},{6,70},{7,71},{8,72},{9,... | collective-permute-start | bytes 393224 | tf_op jit(solution)/shard_map/ppermute | solution.py:8
  52.8 12.9 %collective-permute-start.7 = (bf16[128,512]{1,0:T(8,128)(2,1)S(1)}, bf16[128,512]{1,0:T(8,128)(2,1)S(1)}, u32[]{:S(2)}, u32[]{:S(2)}) collective-permute-start(bf16[128,512]{1,0:T(8,128)(2,1)S(1)} %collective-permute-done.6), channel_id=1, source_target_pairs={{0,128},{1,129},{2,130},{3,131},{4,132},{5,133},{6,134},{7,135},{8... | collective-permute-start | bytes 393224 | tf_op jit(solution)/shard_map/ppermute | solution.py:8
  62.5 10.3 %collective-permute-start.25 = (bf16[128,512]{1,0:T(8,128)(2,1)S(1)}, bf16[128,512]{1,0:T(8,128)(2,1)S(1)}, u32[]{:S(2)}, u32[]{:S(2)}) collective-permute-start(bf16[128,512]{1,0:T(8,128)(2,1)S(1)} %collective-permute-done.24), channel_id=1, source_target_pairs={{0,128},{1,129},{2,130},{3,131},{4,132},{5,133},{6,134},{7,135},{8... | collective-permute-start | bytes 393224 | tf_op jit(solution)/shard_map/ppermute | solution.py:8
  95.8 37.7 %collective-permute-start.26 = (bf16[2,127,1024]{2,1,0:T(8,128)(2,1)}, bf16[2,127,1024]{2,1,0:T(8,128)(2,1)}, u32[]{:S(2)}, u32[]{:S(2)}) collective-permute-start(bf16[2,127,1024]{2,1,0:T(8,128)(2,1)} %bitcast.87), channel_id=1, source_target_pairs={{1,0},{2,1},{3,2},{4,3},{5,4},{6,5},{7,6},{8,7},{9,8},{10,9},{11,1... | collective-permute-start | bytes 1560584 | tf_op jit(solution)/shard_map/ppermute | solution.py:14
  169.3 10.5 %collective-permute-start.9 = (bf16[2,127,1024]{2,1,0:T(8,128)(2,1)S(1)}, bf16[2,127,1024]{2,1,0:T(8,128)(2,1)S(1)}, u32[]{:S(2)}, u32[]{:S(2)}) collective-permute-start(bf16[2,127,1024]{2,1,0:T(8,128)(2,1)S(1)} %slice.145), channel_id=1, source_target_pairs={{0,1},{1,2},{2,3},{3,4},{4,5},{5,6},{6,7},{7,8},{8,9},{9,10},{10,1... | collective-permute-start | bytes 1560584 | tf_op jit(solution)/shard_map/ppermute | solution.py:14
  204.0 196.9 %reduce-scatter.8.cloned.1.call-start = ((), (), s32[]{:S(2)}) async-start(), calls=%async_computation.6 | async-start | bytes 2228224 | tf_op jit(solution)/shard_map/reduce_scatter | solution.py:91
  205.9 206.4 %reduce-scatter.6.cloned.1.call-start = ((), (), s32[]{:S(2)}) async-start(), calls=%async_computation.5 | async-start | bytes 6684672 | tf_op jit(solution)/shard_map/reduce_scatter | solution.py:90
  215.3 370.7 %all-reduce.7.cloned.1.call-start = ((), (), s32[]{:S(2)}) async-start(), calls=%async_computation.8 | async-start | bytes 1048576 | tf_op jit(solution)/shard_map/psum | solution.py:95
  223.1 7.0 %collective-permute-start.11 = (bf16[128,512]{1,0:T(8,128)(2,1)S(1)}, bf16[128,512]{1,0:T(8,128)(2,1)S(1)}, u32[]{:S(2)}, u32[]{:S(2)}) collective-permute-start(bf16[128,512]{1,0:T(8,128)(2,1)S(1)} %collective-permute-done.10), channel_id=1, source_target_pairs={{0,2},{1,3},{2,0},{3,1},{4,6},{5,7},{6,4},{7,5},{8,10},{9,11},{10,... | collective-permute-start | bytes 393224 | tf_op jit(solution)/shard_map/ppermute | solution.py:8
  224.4 11.8 %collective-permute-start.29 = (bf16[128,512]{1,0:T(8,128)(2,1)S(1)}, bf16[128,512]{1,0:T(8,128)(2,1)S(1)}, u32[]{:S(2)}, u32[]{:S(2)}) collective-permute-start(bf16[128,512]{1,0:T(8,128)(2,1)S(1)} %collective-permute-done.28), channel_id=1, source_target_pairs={{0,2},{1,3},{2,0},{3,1},{4,6},{5,7},{6,4},{7,5},{8,10},{9,11},{10,... | collective-permute-start | bytes 393224 | tf_op jit(solution)/shard_map/ppermute | solution.py:8
  230.1 12.1 %collective-permute-start.12 = (bf16[128,512]{1,0:T(8,128)(2,1)S(1)}, bf16[128,512]{1,0:T(8,128)(2,1)S(1)}, u32[]{:S(2)}, u32[]{:S(2)}) collective-permute-start(bf16[128,512]{1,0:T(8,128)(2,1)S(1)} %collective-permute-done.11), channel_id=1, source_target_pairs={{0,4},{1,5},{2,6},{3,7},{4,0},{5,1},{6,2},{7,3},{8,12},{9,13},{10,... | collective-permute-start | bytes 393224 | tf_op jit(solution)/shard_map/ppermute | solution.py:8
  236.2 8.9 %collective-permute-start.30 = (bf16[128,512]{1,0:T(8,128)(2,1)S(1)}, bf16[128,512]{1,0:T(8,128)(2,1)S(1)}, u32[]{:S(2)}, u32[]{:S(2)}) collective-permute-start(bf16[128,512]{1,0:T(8,128)(2,1)S(1)} %collective-permute-done.29), channel_id=1, source_target_pairs={{0,4},{1,5},{2,6},{3,7},{4,0},{5,1},{6,2},{7,3},{8,12},{9,13},{10,... | collective-permute-start | bytes 393224 | tf_op jit(solution)/shard_map/ppermute | solution.py:8
  242.2 47.9 %collective-permute-start.13 = (bf16[128,512]{1,0:T(8,128)(2,1)S(1)}, bf16[128,512]{1,0:T(8,128)(2,1)S(1)}, u32[]{:S(2)}, u32[]{:S(2)}) collective-permute-start(bf16[128,512]{1,0:T(8,128)(2,1)S(1)} %collective-permute-done.12), channel_id=1, source_target_pairs={{0,8},{1,9},{2,10},{3,11},{4,12},{5,13},{6,14},{7,15},{8,0},{9,1},... | collective-permute-start | bytes 393224 | tf_op jit(solution)/shard_map/ppermute | solution.py:8
  245.1 45.0 %collective-permute-start.31 = (bf16[128,512]{1,0:T(8,128)(2,1)S(1)}, bf16[128,512]{1,0:T(8,128)(2,1)S(1)}, u32[]{:S(2)}, u32[]{:S(2)}) collective-permute-start(bf16[128,512]{1,0:T(8,128)(2,1)S(1)} %collective-permute-done.30), channel_id=1, source_target_pairs={{0,8},{1,9},{2,10},{3,11},{4,12},{5,13},{6,14},{7,15},{8,0},{9,1},... | collective-permute-start | bytes 393224 | tf_op jit(solution)/shard_map/ppermute | solution.py:8
  290.1 8.2 %collective-permute-start.14 = (bf16[128,512]{1,0:T(8,128)(2,1)S(1)}, bf16[128,512]{1,0:T(8,128)(2,1)S(1)}, u32[]{:S(2)}, u32[]{:S(2)}) collective-permute-start(bf16[128,512]{1,0:T(8,128)(2,1)S(1)} %collective-permute-done.13), channel_id=1, source_target_pairs={{0,16},{1,17},{2,18},{3,19},{4,20},{5,21},{6,22},{7,23},{8,24},{9,... | collective-permute-start | bytes 393224 | tf_op jit(solution)/shard_map/ppermute | solution.py:8
  290.1 10.1 %collective-permute-start.32 = (bf16[128,512]{1,0:T(8,128)(2,1)S(1)}, bf16[128,512]{1,0:T(8,128)(2,1)S(1)}, u32[]{:S(2)}, u32[]{:S(2)}) collective-permute-start(bf16[128,512]{1,0:T(8,128)(2,1)S(1)} %collective-permute-done.31), channel_id=1, source_target_pairs={{0,16},{1,17},{2,18},{3,19},{4,20},{5,21},{6,22},{7,23},{8,24},{9,... | collective-permute-start | bytes 393224 | tf_op jit(solution)/shard_map/ppermute | solution.py:8
  298.3 99.6 %collective-permute-start.15 = (bf16[128,512]{1,0:T(8,128)(2,1)S(1)}, bf16[128,512]{1,0:T(8,128)(2,1)S(1)}, u32[]{:S(2)}, u32[]{:S(2)}) collective-permute-start(bf16[128,512]{1,0:T(8,128)(2,1)S(1)} %collective-permute-done.14), channel_id=1, source_target_pairs={{0,32},{1,33},{2,34},{3,35},{4,36},{5,37},{6,38},{7,39},{8,40},{9,... | collective-permute-start | bytes 393224 | tf_op jit(solution)/shard_map/ppermute | solution.py:8
  300.2 97.8 %collective-permute-start.33 = (bf16[128,512]{1,0:T(8,128)(2,1)S(1)}, bf16[128,512]{1,0:T(8,128)(2,1)S(1)}, u32[]{:S(2)}, u32[]{:S(2)}) collective-permute-start(bf16[128,512]{1,0:T(8,128)(2,1)S(1)} %collective-permute-done.32), channel_id=1, source_target_pairs={{0,32},{1,33},{2,34},{3,35},{4,36},{5,37},{6,38},{7,39},{8,40},{9,... | collective-permute-start | bytes 393224 | tf_op jit(solution)/shard_map/ppermute | solution.py:8
  397.9 15.0 %collective-permute-start.16 = (bf16[128,512]{1,0:T(8,128)(2,1)S(1)}, bf16[128,512]{1,0:T(8,128)(2,1)S(1)}, u32[]{:S(2)}, u32[]{:S(2)}) collective-permute-start(bf16[128,512]{1,0:T(8,128)(2,1)S(1)} %collective-permute-done.15), channel_id=1, source_target_pairs={{0,64},{1,65},{2,66},{3,67},{4,68},{5,69},{6,70},{7,71},{8,72},{9,... | collective-permute-start | bytes 393224 | tf_op jit(solution)/shard_map/ppermute | solution.py:8
  398.0 20.0 %collective-permute-start.34 = (bf16[128,512]{1,0:T(8,128)(2,1)S(1)}, bf16[128,512]{1,0:T(8,128)(2,1)S(1)}, u32[]{:S(2)}, u32[]{:S(2)}) collective-permute-start(bf16[128,512]{1,0:T(8,128)(2,1)S(1)} %collective-permute-done.33), channel_id=1, source_target_pairs={{0,64},{1,65},{2,66},{3,67},{4,68},{5,69},{6,70},{7,71},{8,72},{9,... | collective-permute-start | bytes 393224 | tf_op jit(solution)/shard_map/ppermute | solution.py:8
  413.0 11.4 %collective-permute-start.17 = (bf16[128,512]{1,0:T(8,128)(2,1)S(1)}, bf16[128,512]{1,0:T(8,128)(2,1)S(1)}, u32[]{:S(2)}, u32[]{:S(2)}) collective-permute-start(bf16[128,512]{1,0:T(8,128)(2,1)S(1)} %collective-permute-done.16), channel_id=1, source_target_pairs={{0,128},{1,129},{2,130},{3,131},{4,132},{5,133},{6,134},{7,135},{8... | collective-permute-start | bytes 393224 | tf_op jit(solution)/shard_map/ppermute | solution.py:8
  418.0 9.5 %collective-permute-start.35 = (bf16[128,512]{1,0:T(8,128)(2,1)S(1)}, bf16[128,512]{1,0:T(8,128)(2,1)S(1)}, u32[]{:S(2)}, u32[]{:S(2)}) collective-permute-start(bf16[128,512]{1,0:T(8,128)(2,1)S(1)} %collective-permute-done.34), channel_id=1, source_target_pairs={{0,128},{1,129},{2,130},{3,131},{4,132},{5,133},{6,134},{7,135},{8... | collective-permute-start | bytes 393224 | tf_op jit(solution)/shard_map/ppermute | solution.py:8
  (35 other events, 280.2 us)
Sparse Core Ops, SparseCore 0:
  9.8 42.0 all-gather.2
  53.8 39.2 all-gather.4
  204.1 65.5 reduce-scatter.9
  272.3 64.3 reduce-scatter.7
  339.3 73.0 reduce-scatter.5
  415.1 170.9 all-reduce.6
where the time goes:
time: 608 us; the launch traced here: 596 us
  waiting for transfers between devices  226 us (37%)
  local copies, waits for them, and re-layouts  130 us (21%)
  blocking collectives  95 us (16%)
  starting transfers between devices  77.5 us (13%)
  other arithmetic  31.2 us (5%)
  matrix products  21.2 us (3%)
  between operations  15.6 us (3%)
    psum x1, waiting for transfers between devices, reduce_terms(): return lax.psum((shares[0], shares[1], shares[2], shares[3]), 'seq')  158 us
    ppermute x32, starting transfers between devices, swapped(): lax.ppermute(shard, axis, [(i, i ^ 1 << distance) for i in range(lax.axis...  68.6 us
    unnamed x1, blocking collectives  51.1 us
    psum x1, blocking collectives, reduce_terms(): return lax.psum((shares[0], shares[1], shares[2], shares[3]), 'seq')  43.9 us
    ppermute x32, waiting for transfers between devices, swapped(): lax.ppermute(shard, axis, [(i, i ^ 1 << distance) for i in range(lax.axis...  31.6 us
    unnamed x60, local copies, waits for them, and re-layouts  22.1 us
    reshape x1, local copies, waits for them, and re-layouts, toeplitz_table(): repeated[:, :filter_tap_count * (3 * filter_tap_count - 1)]  16.5 us
    reshape x1, local copies, waits for them, and re-layouts, unskew(): padded.reshape(group_count, filter_tap_count * (3 * filter_tap_count - 1))  14.1 us
  transfers between devices with their start and end apart: 42, of which 19 were waited for; matrix products, arithmetic and copies ran while one was open for 19% of the time, Pallas kernels for 0%

commit v1 on v0

v1 whole, which is shorter than its diff:
```python
import functools

import jax
import jax.numpy as jnp
from jax import lax
from jax.experimental import pallas as pl
from jax.experimental.pallas import tpu as pltpu
from jax.sharding import PartitionSpec as P

F32 = jnp.float32
BF16 = jnp.bfloat16
NN = (((1,), (0,)), ((), ()))
NT = (((1,), (1,)), ((), ()))
TN = (((0,), (0,)), ((), ()))


def mm(a, b, dims=NN):
    return lax.dot_general(a, b, dims, preferred_element_type=F32)


def lane_group(shape):
    return (lax.broadcasted_iota(jnp.int32, shape, 1) % 128) // 16


def build_tables(filters, TF, TB):
    t = lax.broadcasted_iota(jnp.int32, (128, 256), 0)
    k = lax.broadcasted_iota(jnp.int32, (128, 256), 1)
    to_f = jnp.where(t + k == 128, 1.0, 0.0).astype(BF16)
    to_b = jnp.where(t == k, 1.0, 0.0).astype(BF16)
    pat_f = mm(filters, to_f)
    pat_b = mm(filters, to_b)
    for g in range(32):
        for pat, table in ((pat_f, TF), (pat_b, TB)):
            rows = jnp.broadcast_to(pat[g:g + 1], (128, 256))
            skewed = pltpu.roll(rows, 0, 1, stride=1, stride_axis=0)
            table[g // 8, pl.ds((g % 8) * 128, 128), :] = skewed.astype(BF16)


def anti_identity(n):
    r = lax.broadcasted_iota(jnp.int32, (n, n), 0)
    c = lax.broadcasted_iota(jnp.int32, (n, n), 1)
    return jnp.where(r + c == n - 1, 1.0, 0.0).astype(BF16)


def diag(products, rows):
    group = lane_group((rows, products.shape[1]))
    out = products[0:rows]
    for g in range(1, 8):
        out = jnp.where(group == g, products[g * rows:(g + 1) * rows], out)
    return out


def shifted(x, j):
    if j == 0:
        return x
    return pltpu.roll(x, j % x.shape[0], 0)


def compute_chunk(k, U, C, Win, Wout, taps_ref, TF, TB, UT, HID, GP, PIN, PSH, PFIL):
    w = Win[k]
    wo = Wout[pl.ds(pl.multiple_of(128 * k, 128), 128), :]
    taps = taps_ref[k]
    tf = TF[k]
    tb = TB[k]
    proj, gated, gc, keys, values, queries, ghs = [], [], [], [], [], [], []
    for s in range(2):
        sign = 1 if s == 0 else -1
        kv_at = 0 if s == 0 else 128
        q_at = 128 - kv_at
        pkv = mm(U[s, pl.ds(kv_at, 416), :], w[:, 128:]).astype(BF16)
        pq = mm(U[s, pl.ds(q_at, 416), :], w[:, :128]).astype(BF16)
        gh = mm(C[s], wo, NT).astype(BF16).astype(F32)
        pkv32 = pkv.astype(F32)
        pq32 = pq.astype(F32)
        mkv = jnp.zeros((416, 256), F32)
        mq = jnp.zeros((416, 128), F32)
        for j in range(4):
            mkv = mkv + taps[j:j + 1, 128:] * shifted(pkv32, sign * j)
            mq = mq + taps[j:j + 1, :128] * shifted(pq32, sign * j)
        key, value = mkv[:, :128], mkv[:, 128:]
        gated.append((key * value).astype(BF16))
        keys.append(key)
        values.append(value)
        queries.append(mq)
        ghs.append(gh)
        at = 16 if s == 0 else 0
        gc.append((gh * mq[at:at + 400]).astype(BF16))
        own_kv = 144 if s == 0 else 16
        own_q = 160 - own_kv
        proj.append((pq32[own_q:own_q + 256], pkv32[own_kv:own_kv + 256]))
    wf = jnp.concatenate([gated[0][:400], gc[1]], axis=1)
    f_parts, b_parts = [], []
    prods = None
    for blk in range(2):
        xf = wf[16 + 128 * blk:272 + 128 * blk]
        f_parts.append(diag(mm(tf, xf), 128))
        xb = jnp.concatenate([gc[0][128 * blk:128 * blk + 256], gated[1][16 + 128 * blk:272 + 128 * blk]], axis=1)
        b_parts.append(diag(mm(tb, xb), 128))
        left = jnp.concatenate([gc[0][128 * blk:128 * blk + 128], gated[1][16 + 128 * blk:144 + 128 * blk]], axis=1)
        left = mm(anti_identity(128), left).astype(BF16)
        group = lane_group((128, 256))
        masked = jnp.concatenate([jnp.where(group == g, left, jnp.zeros_like(left)) for g in range(8)], axis=0)
        term = mm(masked, xf, NT)
        prods = term if prods is None else prods + term
    tf3 = tf.reshape(8, 128, 256)
    tb3 = tb.reshape(8, 128, 256)
    f_last = tf3[:, 112:].reshape(128, 256)
    f_first = tf3[:, :16].reshape(128, 256)
    b_last = tb3[:, 112:].reshape(128, 256)
    b_first = tb3[:, :16].reshape(128, 256)
    conv0_x = diag(mm(f_last, gated[0][160:416]), 16)
    gg1_x = diag(mm(f_first, gc[1][0:256]), 16)
    gg0_x = diag(mm(b_last, gc[0][144:400]), 16)
    conv1_x = diag(mm(b_first, gated[1][0:256]), 16)
    conv = [
        jnp.concatenate([f_parts[0][:, :128], f_parts[1][:, :128], conv0_x], axis=0),
        jnp.concatenate([conv1_x, b_parts[0][:, 128:], b_parts[1][:, 128:]], axis=0),
    ]
    gg = [
        jnp.concatenate([b_parts[0][:, :128], b_parts[1][:, :128], gg0_x], axis=0),
        jnp.concatenate([gg1_x, f_parts[0][:, 128:], f_parts[1][:, 128:]], axis=0),
    ]
    short = [jnp.zeros((1, 384), F32) for _ in range(4)]
    for s in range(2):
        sign = 1 if s == 0 else -1
        own = 0 if s == 0 else 16
        q_at = 16 if s == 0 else 128
        kv_at = 144 if s == 0 else 0
        gh_at = 0 if s == 0 else 128
        query = queries[s][q_at:q_at + 272]
        hidden = (query[own:own + 256] * conv[s][own:own + 256]).astype(BF16)
        HID[k, pl.ds(256 * s, 256), :] = hidden
        gm = jnp.concatenate(
            [
                ghs[s][gh_at:gh_at + 272] * conv[s],
                gg[s] * values[s][kv_at:kv_at + 272],
                gg[s] * keys[s][kv_at:kv_at + 272],
            ],
            axis=1,
        ).astype(BF16).astype(F32)
        p_own = jnp.concatenate(proj[s], axis=1)
        total = jnp.zeros((256, 384), F32)
        for j in range(4):
            moved = shifted(gm, -sign * j)[own:own + 256]
            total = total + taps[j:j + 1] * moved
            short[j] = short[j] + jnp.sum(p_own * moved, axis=0, keepdims=True)
        GP[k, pl.ds(256 * s, 256), :] = total.astype(BF16)
    PSH[k] = jnp.concatenate(short, axis=0)
    PIN[k] = mm(UT[...], GP[k])
    rows = []
    for g in range(8):
        r = pltpu.roll(prods[128 * g:128 * g + 128], 129, 1, stride=1, stride_axis=0)
        rows.append(jnp.sum(r, axis=0, keepdims=True))
    PFIL[k] = jnp.concatenate(rows, axis=0)


MESH = pl.DeviceIdType.MESH


def remote(src, dst, send, recv, device):
    copy = pltpu.make_async_remote_copy(
        src_ref=src, dst_ref=dst, send_sem=send, recv_sem=recv, device_id=device, device_id_type=MESH
    )
    copy.start()
    return copy


def wait_bytes(ref, sem):
    pltpu.make_async_copy(ref, ref, sem).wait()


def at_coords(x, y, z, c):
    return ((z // 2) * 4 + x, (z % 2) * 8 + y * 2 + c)


def at_chip(p, c):
    return (p // 8, (p % 8) * 2 + c)


def halves(tile, other):
    lane = lax.broadcasted_iota(jnp.int32, tile.shape, 1)
    low = jnp.where(lane < 64, tile, pltpu.roll(other, 64, 1))
    high = jnp.where(lane < 64, pltpu.roll(tile, 64, 1), other)
    return low, high


def kernel(
    scale,
    strands, cotangent, proj_in, proj_out, taps_ref, filters_ref,
    out_ref, grad_ref, gin_ref, gout_ref, gshort_ref, gfil_ref,
    U, C, W, WO, WSEND, TF, TB, UT, HID, GP, PIN, PSH, PFIL, PART, OUTP, RP,
    SZ, RZ, SXY, RXY, S2, ZH, FIN, FSEND,
    SZ4, RZ4, SXY4, RXY4, S24, ZH4, FIN4, FSEND4, SMALL,
    pair_send, pair_recv, halo_send, halo_recv, fwd_send, fwd_recv,
    w_send, w_recv, wp_send, wp_recv,
    z_send, z_recv, xy_send, xy_recv, zh_send, zh_recv, xg_send, xg_recv, sm_send, sm_recv, op_send, op_recv,
):
    seq, ch = lax.axis_index("seq"), lax.axis_index("ch")
    z_hi, x = seq // 4, seq % 4
    z_lo, y, c = ch // 8, (ch // 2) % 4, ch % 2
    z = z_hi * 2 + z_lo
    b = z_lo * 4 + y
    chip = seq * 8 + b
    before, after = (chip + 127) % 128, (chip + 1) % 128
    partner = at_coords(x, y, z, 1 - c)
    y_up, y_down = at_coords(x, (y + 1) % 4, z, c), at_coords(x, (y + 3) % 4, z, c)
    z_up, z_down = at_coords(x, y, (z + 1) % 8, c), at_coords(x, y, (z + 7) % 8, c)

    barrier = pltpu.get_barrier_semaphore()
    peers = [partner, z_up, z_down]
    for dx in range(4):
        for dy in range(4):
            if dx or dy:
                peers.append(at_coords((x + dx) % 4, (y + dy) % 4, z, c))
    for d in range(1, 4):
        peers.append(at_coords(x, y, (z + 2 * d) % 8, c))
        peers.append(at_coords((x + d) % 4, y, z, 1 - c))
    for q in (before, after):
        peers.append(at_chip(q, 0))
        peers.append(at_chip(q, 1))
    for peer in peers:
        pl.semaphore_signal(barrier, inc=1, device_id=peer, device_id_type=MESH)

    flip = anti_identity(512)
    own = pl.multiple_of(144 + 128 * c, 16)
    own_c0 = pl.multiple_of(128 * c, 16)
    U[0, pl.ds(own, 128), :] = strands[0]
    U[1, pl.ds(own, 128), :] = mm(strands[1], flip).astype(BF16)
    C[0, pl.ds(own_c0, 128), :] = cotangent[0]
    C[1, pl.ds(own, 128), :] = mm(cotangent[1], flip).astype(BF16)
    my_rows = pl.multiple_of(64 * b + 32 * c, 32)
    for k in range(4):
        for s in range(3):
            left = proj_in[:, pl.ds(s * 1024 + k * 256, 128)].astype(F32)
            right = proj_in[:, pl.ds(s * 1024 + k * 256 + 128, 128)].astype(F32)
            even, odd = halves(left, right)
            first = c == 0
            W[k, pl.ds(my_rows, 32), pl.ds(128 * s, 128)] = jnp.where(first, even, odd).astype(BF16)
            WSEND[k, :, pl.ds(128 * s, 128)] = jnp.where(first, odd, even).astype(BF16)
    WO[pl.ds(pl.multiple_of(64 * b, 64), 64), :] = proj_out[...]
    pl.semaphore_wait(barrier, len(peers))

    wp = [
        remote(WSEND.at[k], W.at[k, pl.ds(my_rows, 32), :], wp_send.at[k], wp_recv.at[k], partner) for k in range(4)
    ]
    far = jnp.where(c == 0, before, after)
    near = jnp.where(c == 0, after, before)
    big_at = pl.multiple_of(jnp.where(c == 0, 400, 16), 16)
    small_src = pl.multiple_of(own + jnp.where(c == 0, 112, 0), 16)
    small_at = pl.multiple_of(jnp.where(c == 0, 0, 528), 16)
    halo = []
    for s in range(2):
        halo.append(remote(
            U.at[s, pl.ds(own, 128), :], U.at[s, pl.ds(big_at, 128), :],
            halo_send.at[s], halo_recv.at[1 - c], at_chip(far, s)))
        halo.append(remote(
            U.at[s, pl.ds(small_src, 16), :], U.at[s, pl.ds(small_at, 16), :],
            halo_send.at[2 + s], halo_recv.at[2 + c], at_chip(near, s)))
    c_own = pl.multiple_of(jnp.where(c == 0, 0, 272), 16)
    c_big = pl.multiple_of(jnp.where(c == 0, 256, 16), 16)
    halo.append(remote(
        C.at[c, pl.ds(c_own, 128), :], C.at[c, pl.ds(c_big, 128), :],
        halo_send.at[4], halo_recv.at[4], at_chip(far, c)))
    c_small_src = pl.multiple_of(jnp.where(c == 0, 144 + 112, 128), 16)
    c_small = pl.multiple_of(jnp.where(c == 0, 0, 384), 16)
    halo.append(remote(
        C.at[1 - c, pl.ds(c_small_src, 16), :], C.at[1 - c, pl.ds(c_small, 16), :],
        halo_send.at[5], halo_recv.at[5], at_chip(near, 1 - c)))
    pair = [
        remote(U.at[s, pl.ds(own, 128), :], U.at[s, pl.ds(own, 128), :], pair_send.at[s], pair_recv.at[s], partner)
        for s in range(2)
    ]
    pair.append(remote(
        C.at[0, pl.ds(own_c0, 128), :], C.at[0, pl.ds(own_c0, 128), :], pair_send.at[2], pair_recv.at[2], partner))
    pair.append(remote(
        C.at[1, pl.ds(own, 128), :], C.at[1, pl.ds(own, 128), :], pair_send.at[3], pair_recv.at[3], partner))

    def shard(m, yy, zz, half=None):
        at, size = 64 * (zz * 4 + yy), 64
        if half is not None:
            at, size = at + 32 * half, 32
        rows = pl.ds(pl.multiple_of(at, 32), size)
        return WO.at[rows, :] if m == 4 else W.at[m, rows, :]

    y_next, y_prev, y_far = (y + 1) % 4, (y + 3) % 4, (y + 2) % 4
    order = (0, 4, 1, 2, 3)

    def gather_first(m):
        mine = shard(m, y, z_lo)
        remote(mine, mine, w_send.at[m], w_recv.at[m, 0], y_up)
        remote(mine, mine, w_send.at[m], w_recv.at[m, 1], y_down)
        low, high = shard(m, y, z_lo, 0), shard(m, y, z_lo, 1)
        remote(low, low, w_send.at[m], w_recv.at[m, 4], z_up)
        remote(high, high, w_send.at[m], w_recv.at[m, 4], z_down)

    def gather_second(m):
        wait_bytes(shard(m, y_prev, z_lo), w_recv.at[m, 0])
        wait_bytes(shard(m, y_next, z_lo), w_recv.at[m, 1])
        low, high = shard(m, y_prev, z_lo, 0), shard(m, y_prev, z_lo, 1)
        remote(low, low, w_send.at[m], w_recv.at[m, 2], y_up)
        remote(low, low, w_send.at[m], w_recv.at[m, 4], z_up)
        remote(high, high, w_send.at[m], w_recv.at[m, 4], z_down)
        low, high = shard(m, y_next, z_lo, 0), shard(m, y_next, z_lo, 1)
        remote(high, high, w_send.at[m], w_recv.at[m, 3], y_down)
        remote(low, low, w_send.at[m], w_recv.at[m, 4], z_up)
        remote(high, high, w_send.at[m], w_recv.at[m, 4], z_down)

    def gather_third(m):
        low, high = shard(m, y_far, z_lo, 0), shard(m, y_far, z_lo, 1)
        wait_bytes(low, w_recv.at[m, 2])
        remote(low, low, w_send.at[m], w_recv.at[m, 4], z_up)
        wait_bytes(high, w_recv.at[m, 3])
        remote(high, high, w_send.at[m], w_recv.at[m, 4], z_down)

    def gather_last(m):
        rows = WO if m == 4 else W.at[m]
        wait_bytes(rows.at[pl.ds(0, 256), :], w_recv.at[m, 4])

    def gather_sent(m):
        rows = WO if m == 4 else W.at[m]
        wait_bytes(rows.at[pl.ds(0, 448), :], w_send.at[m])

    for m in order:
        if m < 4:
            wp[m].wait()
        gather_first(m)

    build_tables(filters_ref[...], TF, TB)

    for m in order:
        gather_second(m)
    wait_bytes(U.at[c, pl.ds(16, 128), :], halo_recv.at[0])
    wait_bytes(U.at[c, pl.ds(400, 128), :], halo_recv.at[1])
    wait_bytes(U.at[c, pl.ds(0, 16), :], halo_recv.at[2])
    wait_bytes(U.at[c, pl.ds(528, 16), :], halo_recv.at[3])
    wait_bytes(C.at[c, pl.ds(c_big, 128), :], halo_recv.at[4])
    wait_bytes(C.at[c, pl.ds(pl.multiple_of(jnp.where(c == 0, 384, 0), 16), 16), :], halo_recv.at[5])
    c_halo = pl.multiple_of(jnp.where(c == 0, 256, 0), 16)
    c_halo_other = pl.multiple_of(jnp.where(c == 0, 0, 256), 16)
    fwd = []
    for i, at in enumerate((0, 400)):
        rows = U.at[c, pl.ds(at, 144), :]
        fwd.append(remote(rows, rows, fwd_send.at[i], fwd_recv.at[i], partner))
    rows = C.at[c, pl.ds(c_halo, 144), :]
    fwd.append(remote(rows, rows, fwd_send.at[2], fwd_recv.at[2], partner))
    for m in order:
        gather_third(m)
    for copy in pair:
        copy.wait()
    for copy in halo:
        copy.wait_send()
    for i, at in enumerate((0, 400)):
        wait_bytes(U.at[1 - c, pl.ds(at, 144), :], fwd_recv.at[i])
    wait_bytes(C.at[1 - c, pl.ds(c_halo_other, 144), :], fwd_recv.at[2])
    for copy in fwd:
        copy.wait_send()

    @pl.when(chip == 0)
    def _():
        U[:, pl.ds(0, 144), :] = jnp.zeros((2, 144, 512), BF16)
        C[1, pl.ds(0, 144), :] = jnp.zeros((144, 512), BF16)

    @pl.when(chip == 127)
    def _():
        U[:, pl.ds(400, 144), :] = jnp.zeros((2, 144, 512), BF16)
        C[0, pl.ds(256, 144), :] = jnp.zeros((144, 512), BF16)

    for s in range(2):
        UT[:, pl.ds(256 * s, 256)] = jnp.transpose(U[s, pl.ds(144, 256), :])
    for m in order:
        gather_last(m)
        gather_sent(m)

    def stages(part, sz, rz, sxy, rxy, s2, zh, fsend, width, base):
        def z_start(k):
            rows = pl.ds(pl.multiple_of((1 - z_lo) * 256, 256), 256)
            sz[k] = part(k, rows).astype(BF16).reshape(4, 2, 32, width)
            remote(sz.at[k, :, 0], rz.at[k, :, 0], z_send.at[base + k], z_recv.at[base + k, 0], z_up)
            remote(sz.at[k, :, 1], rz.at[k, :, 1], z_send.at[base + k], z_recv.at[base + k, 1], z_down)

        def xy_start(k):
            wait_bytes(rz.at[k, :, 0], z_recv.at[base + k, 0])
            wait_bytes(rz.at[k, :, 1], z_recv.at[base + k, 1])
            wait_bytes(sz.at[k], z_send.at[base + k])
            rows = pl.ds(pl.multiple_of(z_lo * 256, 256), 256)
            total = part(k, rows) + rz[k].astype(F32).reshape(256, width)
            sxy[k] = total.astype(BF16).reshape(4, 4, 16, width)
            for dx in range(4):
                for dy in range(4):
                    if dx or dy:
                        xx, yy = (x + dx) % 4, (y + dy) % 4
                        remote(sxy.at[k, yy, xx], rxy.at[k, 4 * dx + dy - 1],
                               xy_send.at[base + k], xy_recv.at[base + k], at_coords(xx, yy, z, c))

        def zh_start(k):
            wait_bytes(rxy.at[k], xy_recv.at[base + k])
            wait_bytes(rxy.at[k], xy_send.at[base + k])
            total = sxy[k, y, x].astype(F32)
            for i in range(15):
                total = total + rxy[k, i].astype(F32)
            zh[k, z_hi] = total.astype(BF16)
            for d in range(1, 4):
                remote(zh.at[k, z_hi], zh.at[k, z_hi], zh_send.at[base + k], zh_recv.at[base + k],
                       at_coords(x, y, (z + 2 * d) % 8, c))

        def zh_end(k):
            wait_bytes(zh.at[k, pl.ds(0, 3)], zh_recv.at[base + k])
            wait_bytes(zh.at[k, pl.ds(0, 3)], zh_send.at[base + k])
            total = zh[k, 0].astype(F32)
            for i in range(1, 4):
                total = total + zh[k, i].astype(F32)
            fsend[k] = total * scale

        return z_start, xy_start, zh_start, zh_end

    in_z, in_xy, in_zh, in_end = stages(
        lambda k, rows: PIN[k, rows, :], SZ, RZ, SXY, RXY, S2, ZH, FSEND, 384, 0)
    out_z, out_xy, out_zh, out_end = stages(
        lambda k, rows: PART[rows, :], SZ4, RZ4, SXY4, RXY4, S24, ZH4, FSEND4, 640, 4)

    target = x // 2
    row_at = pl.multiple_of(16 * (x % 2), 16)

    def in_gather(k):
        in_end(k)
        place = FIN.at[k, c, pl.ds(row_at, 16), :]
        for d in range(1, 4):
            remote(FSEND.at[k], place, xg_send.at[k], xg_recv.at[k], at_coords((x + d) % 4, y, z, target))

        @pl.when(c == target)
        def _():
            pltpu.make_async_copy(FSEND.at[k], place, xg_recv.at[k]).start()

        @pl.when(c != target)
        def _():
            remote(FSEND.at[k], place, xg_send.at[k], xg_recv.at[k], partner)

    def in_last(k):
        wait_bytes(FIN.at[k], xg_recv.at[k])
        wait_bytes(FSEND.at[pl.ds(0, 3)], xg_send.at[k])

        @pl.when(c != target)
        def _():
            wait_bytes(FSEND.at[k], xg_send.at[k])

        for s in range(3):
            low, high = halves(FIN[k, 0, :, pl.ds(128 * s, 128)], FIN[k, 1, :, pl.ds(128 * s, 128)])
            gin_ref[:, pl.ds(s * 1024 + k * 256, 128)] = low
            gin_ref[:, pl.ds(s * 1024 + k * 256 + 128, 128)] = high

    def out_gather():
        out_end(0)
        place = FIN4.at[x]
        for d in range(1, 4):
            remote(FSEND4.at[0], place, xg_send.at[4], xg_recv.at[4], at_coords((x + d) % 4, y, z, c))

        @pl.when(x == 0)
        def _():
            small = FSEND4.at[0, :, pl.ds(512, 128)]
            for d in range(1, 4):
                remote(small, SMALL, sm_send, sm_recv, at_coords((x + d) % 4, y, z, 1 - c))
            remote(small, SMALL, sm_send, sm_recv, partner)

        FIN4[x] = FSEND4[0]

    def out_last():
        wait_bytes(FIN4.at[pl.ds(0, 3)], xg_recv.at[4])
        wait_bytes(FIN4.at[pl.ds(0, 3)], xg_send.at[4])
        wait_bytes(SMALL, sm_recv)

        @pl.when(x == 0)
        def _():
            wait_bytes(FIN4.at[0, :, pl.ds(0, 512)], sm_send)

        gout_ref[...] = FIN4[...].reshape(64, 640)[:, :512]
        mine = FIN4[0, :, pl.ds(512, 128)]
        theirs = SMALL[...]
        reversal = anti_identity(128).astype(F32)
        gfil_ref[...] = lax.dot_general(
            mine, reversal, NN, precision=lax.Precision.HIGHEST, preferred_element_type=F32)[8:12]
        even = jnp.where(c == 0, mine, theirs)
        odd = jnp.where(c == 0, theirs, mine)
        lane = lax.broadcasted_iota(jnp.int32, (4, 128), 1)

        def blocks(v):
            a, t = v[0:4], v[4:8]
            shifted_a, shifted_t = pltpu.roll(a, 64, 1), pltpu.roll(t, 64, 1)
            first = jnp.where(b % 2 == 0, a, shifted_a)
            second = jnp.where(b % 2 == 0, shifted_a, t)
            third = jnp.where(b % 2 == 0, t, shifted_t)
            return first, second, third

        e, o = blocks(even), blocks(odd)
        one = jnp.where(c == 0, e[0], o[1])
        two = jnp.where(c == 0, o[0], e[2])
        three = jnp.where(c == 0, e[1], o[2])
        left = jnp.where(lane < 64, one, pltpu.roll(two, 64, 1))
        pad = jnp.zeros((124, 128), F32)
        gshort_ref[pl.ds(0, 128), :] = jnp.transpose(jnp.concatenate([left, pad], axis=0))[:, :4]
        gshort_ref[pl.ds(128, 64), :] = jnp.transpose(jnp.concatenate([three, pad], axis=0))[:64, :4]

    def body(k, carry):
        compute_chunk(k, U, C, W, WO, taps_ref, TF, TB, UT, HID, GP, PIN, PSH, PFIL)
        in_z(k)

        @pl.when(k >= 1)
        def _():
            in_xy(k - 1)

        @pl.when(k >= 2)
        def _():
            in_zh(k - 2)

        @pl.when(k >= 3)
        def _():
            in_gather(k - 3)

        return carry

    lax.fori_loop(0, 4, body, 0)

    for k in range(4):
        rows = pl.ds(128 * k, 128)
        part = mm(HID[k, pl.ds(0, 256), :], C[0, pl.ds(0, 256), :], TN)
        PART[rows, pl.ds(0, 512)] = part + mm(HID[k, pl.ds(256, 256), :], C[1, pl.ds(144, 256), :], TN)
    PART[:, pl.ds(512, 128)] = jnp.zeros((512, 128), F32)
    for i in range(8):
        m = i // 2
        tiles = (3 * m, 3 * m + 1) if i % 2 == 0 else (3 * m + 1, 3 * m + 2)
        pieces = [PSH[t % 4, :, pl.ds(128 * (t // 4), 128)] for t in tiles]
        taps_first = pltpu.roll(PFIL[m], 255, 1)[4 * (i % 2):4 * (i % 2) + 4, :128]
        PART[pl.ds(64 * i, 16), pl.ds(512, 128)] = jnp.concatenate(
            pieces + [taps_first, jnp.zeros((4, 128), F32)], axis=0)
    out_z(0)
    in_xy(3)
    in_zh(2)
    in_gather(1)
    res = mm(HID[0], WO[pl.ds(0, 128), :])
    for k in range(1, 4):
        res = res + mm(HID[k], WO[pl.ds(128 * k, 128), :])
    OUTP[0] = res
    out_xy(0)
    in_zh(3)
    in_gather(2)
    res = mm(GP[0], W[0], NT)
    for k in range(1, 4):
        res = res + mm(GP[k], W[k], NT)
    OUTP[1] = res
    other_rows = 128 * (1 - c)
    op = []
    for o in range(2):
        for s in range(2):
            rows = pl.ds(pl.multiple_of(256 * s + other_rows, 128), 128)
            op.append(remote(OUTP.at[o, rows, :], RP.at[o, s], op_send.at[o, s], op_recv.at[o, s], partner))
    out_zh(0)
    in_gather(3)
    out_gather()
    for copy in op:
        copy.wait()
    for o, ref in enumerate((out_ref, grad_ref)):
        for s in range(2):
            rows = pl.ds(pl.multiple_of(256 * s + 128 * c, 128), 128)
            value = (OUTP[o, rows, :] + RP[o, s]).astype(BF16)
            ref[s] = value if s == 0 else mm(value, flip).astype(BF16)
    for k in range(4):
        in_last(k)
    out_last()


def shards(strands, cotangent, proj_in, proj_out, short_taps, filters):
    c = lax.axis_index("ch") % 2
    taps = lax.dynamic_index_in_dim(short_taps.reshape(3, 8, 2, 64, 4), c, 2, keepdims=False)
    taps = taps.reshape(3, 4, 128, 4).transpose(1, 3, 0, 2).reshape(4, 4, 384)
    fil = lax.dynamic_index_in_dim(filters.reshape(8, 2, 4, 128), c, 1, keepdims=False).reshape(32, 128)
    length = strands.shape[1] * lax.axis_size(("seq", "ch"))
    scale = float(length) ** (-0.5)
    vmem = pl.BlockSpec(memory_space=pltpu.VMEM)
    dma = pltpu.SemaphoreType.DMA
    outs = (
        jax.ShapeDtypeStruct((2, 128, 512), BF16),
        jax.ShapeDtypeStruct((2, 128, 512), BF16),
        jax.ShapeDtypeStruct((32, 3072), F32),
        jax.ShapeDtypeStruct((64, 512), F32),
        jax.ShapeDtypeStruct((192, 4), F32),
        jax.ShapeDtypeStruct((4, 128), F32),
    )
    scratch = [
        pltpu.VMEM((2, 544, 512), BF16),
        pltpu.VMEM((2, 400, 512), BF16),
        pltpu.VMEM((4, 512, 384), BF16),
        pltpu.VMEM((512, 512), BF16),
        pltpu.VMEM((4, 32, 384), BF16),
        pltpu.VMEM((4, 1024, 256), BF16),
        pltpu.VMEM((4, 1024, 256), BF16),
        pltpu.VMEM((512, 512), BF16),
        pltpu.VMEM((4, 512, 128), BF16),
        pltpu.VMEM((4, 512, 384), BF16),
        pltpu.VMEM((4, 512, 384), F32),
        pltpu.VMEM((4, 4, 384), F32),
        pltpu.VMEM((4, 8, 256), F32),
        pltpu.VMEM((512, 640), F32),
        pltpu.VMEM((2, 512, 512), F32),
        pltpu.VMEM((2, 2, 128, 512), F32),
    ]
    for n, width in ((4, 384), (1, 640)):
        scratch += [
            pltpu.VMEM((n, 4, 2, 32, width), BF16),
            pltpu.VMEM((n, 4, 2, 32, width), BF16),
            pltpu.VMEM((n, 4, 4, 16, width), BF16),
            pltpu.VMEM((n, 15, 16, width), BF16),
            pltpu.VMEM((8, 128), F32),
            pltpu.VMEM((n, 4, 16, width), BF16),
            pltpu.VMEM((4, 2, 32, 384) if n == 4 else (4, 16, 640), F32),
            pltpu.VMEM((n, 16, width), F32),
        ]
    scratch.append(pltpu.VMEM((16, 128), F32))
    scratch += [
        dma((4,)), dma((4,)), dma((6,)), dma((6,)), dma((3,)), dma((3,)),
        dma((5,)), dma((5, 5)), dma((4,)), dma((4,)),
        dma((5,)), dma((5, 2)), dma((5,)), dma((5,)), dma((5,)), dma((5,)), dma((5,)), dma((5,)),
        dma, dma, dma((2, 2)), dma((2, 2)),
    ]
    return pl.pallas_call(
        functools.partial(kernel, scale),
        out_shape=outs,
        in_specs=[vmem] * 6,
        out_specs=tuple([vmem] * 6),
        scratch_shapes=scratch,
        compiler_params=pltpu.CompilerParams(
            collective_id=0, has_side_effects=True, vmem_limit_bytes=58 * 2**20
        ),
        cost_estimate=pl.CostEstimate(flops=9 * 10**9, bytes_accessed=4 * 10**6, transcendentals=0),
    )(strands, cotangent, proj_in, proj_out, taps, fil)


def solution(mesh):
    placed = P(None, ("seq", "ch"), None)
    rows = P("ch", None)
    return jax.shard_map(
        shards,
        mesh=mesh,
        in_specs=(placed, placed, rows, rows, P(), P()),
        out_specs=(placed, placed, rows, rows, rows, rows),
        check_vma=False,
    )
```

time: 608 us -> 83 us (0.14); the launches traced: 596 us -> 82.8 us
  waiting for transfers between devices: 226 us -> 0 us
  local copies, waits for them, and re-layouts: 130 us -> 8.92 us
  blocking collectives: 95 us -> 0 us
  starting transfers between devices: 77.5 us -> 0 us
  Pallas kernels: 0 us -> 73.1 us
  other arithmetic: 31.2 us -> 0 us
  matrix products: 21.2 us -> 0 us
  between operations: 15.6 us -> 0.69 us
    psum x1 -> x0, waiting for transfers between devices: 158 us -> none  [reduce_terms(): return lax.psum((shares[0], shares[1], shares[2], shares[3]), 'seq')]
    ppermute x36 -> x0, starting transfers between devices: 77.3 us -> none  [the longest x32 68.6 us: swapped(): lax.ppermute(shard, axis, [(i, i ^ 1 << distance) for i in range(lax.axis...]
    pallas_call x0 -> x1, Pallas kernels: none -> 73.1 us  [shards(): pl.pallas_call(functools.partial(kernel, scale), out_shape=outs, in_specs...]
    unnamed x1 -> x0, blocking collectives: 51.1 us -> none
    psum x1 -> x0, blocking collectives: 43.9 us -> none  [reduce_terms(): return lax.psum((shares[0], shares[1], shares[2], shares[3]), 'seq')]
    ppermute x36 -> x0, waiting for transfers between devices: 43.6 us -> none  [the longest x32 31.6 us: swapped(): lax.ppermute(shard, axis, [(i, i ^ 1 << distance) for i in range(lax.axis...]
    reshape x6 -> x2, local copies, waits for them, and re-layouts: 40.1 us -> 0.21 us  [the longest x1 0.12 us: shards(): short_taps.reshape(3, 8, 2, 64, 4)]
    rev x9 -> x0, local copies, waits for them, and re-layouts: 28.9 us -> none  [the longest x1 8.9 us: shards(): grad_gated = long_conv(grad_ext, toeplitz, group_size)[:, ::-1]]
  transfers between devices with their start and end apart: 42 -> 0, of which waited for: 19 -> 0; matrix products, arithmetic and copies ran while one was open for 19% -> 0% of each run, Pallas kernels for 0% -> 0%
where the time goes in v1:
time: 83 us; the launch traced here: 82.8 us
  Pallas kernels  73.1 us (88%)
  local copies, waits for them, and re-layouts  8.92 us (11%)
    pallas_call x1, Pallas kernels, shards(): pl.pallas_call(functools.partial(kernel, scale), out_shape=outs, in_specs...  73.1 us
    unnamed x17, local copies, waits for them, and re-layouts  5.77 us

profile of v1, /device:TPU:8, one launch (start us, length us, event | category | flops | bytes accessed | tf_op | source)
XLA Modules:
  0.0 82.8 jit_solution(4673725851563770578)
XLA Ops:
  0.6 0.0 copy-start
  0.6 0.0 copy-start.4
  0.7 0.7 copy-done
  1.4 0.6 constant_dynamic-slice_fusion
  2.0 0.0 copy-done.4
  2.0 0.1 reshape.29
  2.1 0.1 dynamic-slice_reduce_fusion
  2.2 0.1 reshape.34
  2.3 0.6 copy.23
  2.9 73.1 %shard_map.109 = (bf16[2,128,512]{2,1,0:T(8,128)(2,1)}, bf16[2,128,512]{2,1,0:T(8,128)(2,1)}, f32[32,3072]{1,0:T(8,128)}, f32[64,512]{1,0:T(8,128)}, f32[192,4]{1,0:T(8,128)}, /*index=5*/f32[4,128]{1,0:T(4,128)}) custom-call(bf16[2,128,512]{2,1,0:T(8,128)(2,1)} %strands.1, bf16[2,128,512]{2,1,0:T(8,128)(2,1)} %cotangent.1, bf16[32,3072]{1,0:T(8,128)(2,1)} %proj_in.1, ...), custom_call_target="tpu_custom_call" | custom-call | flops 8999999488 | bytes 4000000 | tf_op jit(solution)/shard_map/pallas_call | solution.py:623
  76.1 1.6 %copy.17 = f32[192,4]{0,1:T(4,128)} copy(f32[192,4]{1,0:T(8,128)} %get-tuple-element.16) | data formatting | bytes 6144 | tf_op jit(solution)/shard_map/pallas_call | solution.py:623
  77.7 0.0 copy-start.2
  77.7 1.7 %copy.29 = bf16[2,128,512]{2,1,0:T(8,128)(2,1)} copy(bf16[2,128,512]{2,1,0:T(8,128)(2,1)} %get-tuple-element.24) | data formatting | bytes 524288
  79.4 0.0 copy-done.2
  79.4 0.0 copy-start.1
  79.4 0.7 copy.30
  80.1 0.4 copy-done.1
  80.5 0.0 copy-start.3
  80.5 0.7 copy.31
  81.2 0.3 copy-done.3
  81.5 0.0 copy-start.5
  81.5 0.7 copy.32
  82.2 0.0 copy-done.5
  82.2 0.6 copy.33
Async XLA Ops:
  0.6 0.7 copy-start
  0.6 1.3 %copy-start.4 = (f32[3072,4]{0,1:T(4,128)S(1)}, f32[3072,4]{0,1:T(4,128)}, u32[]{:S(2)}) copy-start(f32[3072,4]{0,1:T(4,128)} %param.10) | copy-start | bytes 147460
  77.7 1.7 %copy-start.2 = (bf16[2,128,512]{2,1,0:T(8,128)(2,1)S(1)}, bf16[2,128,512]{2,1,0:T(8,128)(2,1)}, u32[]{:S(2)}) copy-start(bf16[2,128,512]{2,1,0:T(8,128)(2,1)} %get-tuple-element.25) | copy-start | bytes 786436
  79.4 1.1 %copy-start.1 = (f32[32,3072]{1,0:T(8,128)S(1)}, f32[32,3072]{1,0:T(8,128)}, u32[]{:S(2)}) copy-start(f32[32,3072]{1,0:T(8,128)} %get-tuple-element.26) | copy-start | bytes 1179652
  80.5 1.0 %copy-start.3 = (f32[64,512]{1,0:T(8,128)S(1)}, f32[64,512]{1,0:T(8,128)}, u32[]{:S(2)}) copy-start(f32[64,512]{1,0:T(8,128)} %get-tuple-element.27) | copy-start | bytes 393220
  81.5 0.7 copy-start.5

commit v2 on v1

v2 whole, which is shorter than its diff:
```python
import functools

import jax
import jax.numpy as jnp
from jax import lax
from jax.experimental import pallas as pl
from jax.experimental.pallas import tpu as pltpu
from jax.sharding import PartitionSpec as P

F32 = jnp.float32
BF16 = jnp.bfloat16
NN = (((1,), (0,)), ((), ()))
NT = (((1,), (1,)), ((), ()))
TN = (((0,), (0,)), ((), ()))


def mm(a, b, dims=NN):
    return lax.dot_general(a, b, dims, preferred_element_type=F32)


def lane_group(shape):
    return (lax.broadcasted_iota(jnp.int32, shape, 1) % 128) // 16


def build_tables(filters, TF, TB):
    t = lax.broadcasted_iota(jnp.int32, (128, 256), 0)
    k = lax.broadcasted_iota(jnp.int32, (128, 256), 1)
    to_f = jnp.where(t + k == 128, 1.0, 0.0).astype(BF16)
    to_b = jnp.where(t == k, 1.0, 0.0).astype(BF16)
    pat_f = mm(filters, to_f)
    pat_b = mm(filters, to_b)
    for g in range(32):
        for pat, table in ((pat_f, TF), (pat_b, TB)):
            rows = jnp.broadcast_to(pat[g:g + 1], (128, 256))
            skewed = pltpu.roll(rows, 0, 1, stride=1, stride_axis=0)
            table[g // 8, pl.ds((g % 8) * 128, 128), :] = skewed.astype(BF16)


def anti_identity(n):
    r = lax.broadcasted_iota(jnp.int32, (n, n), 0)
    c = lax.broadcasted_iota(jnp.int32, (n, n), 1)
    return jnp.where(r + c == n - 1, 1.0, 0.0).astype(BF16)


def diag(products, rows):
    group = lane_group((rows, products.shape[1]))
    out = products[0:rows]
    for g in range(1, 8):
        out = jnp.where(group == g, products[g * rows:(g + 1) * rows], out)
    return out


def shifted(x, j):
    if j == 0:
        return x
    return pltpu.roll(x, j % x.shape[0], 0)


def compute_chunk(k, U, C, Win, Wout, taps_ref, TF, TB, UT, HID, GP, PART, PSH, PFIL, hook_a, hook_b):
    w = Win[k]
    wo = Wout[k].reshape(128, 512)
    taps = taps_ref[k]
    tf = TF[k]
    tb = TB[k]
    proj, gated, gc, keys, values, queries, ghs = [], [], [], [], [], [], []
    for s in range(2):
        sign = 1 if s == 0 else -1
        kv_at = 0 if s == 0 else 128
        q_at = 128 - kv_at
        pkv = mm(U[s, pl.ds(kv_at, 416), :], w[:, 128:]).astype(BF16)
        pq = mm(U[s, pl.ds(q_at, 416), :], w[:, :128]).astype(BF16)
        gh = mm(C[s], wo, NT).astype(BF16).astype(F32)
        pkv32 = pkv.astype(F32)
        pq32 = pq.astype(F32)
        mkv = jnp.zeros((416, 256), F32)
        mq = jnp.zeros((416, 128), F32)
        for j in range(4):
            mkv = mkv + taps[j:j + 1, 128:] * shifted(pkv32, sign * j)
            mq = mq + taps[j:j + 1, :128] * shifted(pq32, sign * j)
        key, value = mkv[:, :128], mkv[:, 128:]
        gated.append((key * value).astype(BF16))
        keys.append(key)
        values.append(value)
        queries.append(mq)
        ghs.append(gh)
        at = 16 if s == 0 else 0
        gc.append((gh * mq[at:at + 400]).astype(BF16))
        own_kv = 144 if s == 0 else 16
        own_q = 160 - own_kv
        proj.append((pq32[own_q:own_q + 256], pkv32[own_kv:own_kv + 256]))
    hook_a()
    wf = jnp.concatenate([gated[0][:400], gc[1]], axis=1)
    f_parts, b_parts = [], []
    prods = None
    for blk in range(2):
        xf = wf[16 + 128 * blk:272 + 128 * blk]
        f_parts.append(diag(mm(tf, xf), 128))
        xb = jnp.concatenate([gc[0][128 * blk:128 * blk + 256], gated[1][16 + 128 * blk:272 + 128 * blk]], axis=1)
        b_parts.append(diag(mm(tb, xb), 128))
        left = jnp.concatenate([gc[0][128 * blk:128 * blk + 128], gated[1][16 + 128 * blk:144 + 128 * blk]], axis=1)
        left = mm(anti_identity(128), left).astype(BF16)
        group = lane_group((128, 256))
        masked = jnp.concatenate([jnp.where(group == g, left, jnp.zeros_like(left)) for g in range(8)], axis=0)
        term = mm(masked, xf, NT)
        prods = term if prods is None else prods + term
    tf3 = tf.reshape(8, 128, 256)
    tb3 = tb.reshape(8, 128, 256)
    f_last = tf3[:, 112:].reshape(128, 256)
    f_first = tf3[:, :16].reshape(128, 256)
    b_last = tb3[:, 112:].reshape(128, 256)
    b_first = tb3[:, :16].reshape(128, 256)
    conv0_x = diag(mm(f_last, gated[0][160:416]), 16)
    gg1_x = diag(mm(f_first, gc[1][0:256]), 16)
    gg0_x = diag(mm(b_last, gc[0][144:400]), 16)
    conv1_x = diag(mm(b_first, gated[1][0:256]), 16)
    conv = [
        jnp.concatenate([f_parts[0][:, :128], f_parts[1][:, :128], conv0_x], axis=0),
        jnp.concatenate([conv1_x, b_parts[0][:, 128:], b_parts[1][:, 128:]], axis=0),
    ]
    gg = [
        jnp.concatenate([b_parts[0][:, :128], b_parts[1][:, :128], gg0_x], axis=0),
        jnp.concatenate([gg1_x, f_parts[0][:, 128:], f_parts[1][:, 128:]], axis=0),
    ]
    hook_b()
    short = [jnp.zeros((1, 384), F32) for _ in range(4)]
    for s in range(2):
        sign = 1 if s == 0 else -1
        own = 0 if s == 0 else 16
        q_at = 16 if s == 0 else 128
        kv_at = 144 if s == 0 else 0
        gh_at = 0 if s == 0 else 128
        query = queries[s][q_at:q_at + 272]
        hidden = (query[own:own + 256] * conv[s][own:own + 256]).astype(BF16)
        HID[k, pl.ds(256 * s, 256), :] = hidden
        gm = jnp.concatenate(
            [
                ghs[s][gh_at:gh_at + 272] * conv[s],
                gg[s] * values[s][kv_at:kv_at + 272],
                gg[s] * keys[s][kv_at:kv_at + 272],
            ],
            axis=1,
        ).astype(BF16).astype(F32)
        p_own = jnp.concatenate(proj[s], axis=1)
        total = jnp.zeros((256, 384), F32)
        for j in range(4):
            moved = shifted(gm, -sign * j)[own:own + 256]
            total = total + taps[j:j + 1] * moved
            short[j] = short[j] + jnp.sum(p_own * moved, axis=0, keepdims=True)
        GP[k, pl.ds(256 * s, 256), :] = total.astype(BF16)
    PSH[k] = jnp.concatenate(short, axis=0)
    PART[k, :, :, :, pl.ds(0, 384)] = mm(UT[...], GP[k]).reshape(8, 4, 16, 384)
    po = mm(HID[k, pl.ds(0, 256), :], C[0, pl.ds(0, 256), :], TN)
    po = po + mm(HID[k, pl.ds(256, 256), :], C[1, pl.ds(144, 256), :], TN)
    for q in range(4):
        PART[k, :, q, :, pl.ds(384, 128)] = po[:, 128 * q:128 * q + 128].reshape(8, 16, 128)
    rows = []
    for g in range(8):
        r = pltpu.roll(prods[128 * g:128 * g + 128], 129, 1, stride=1, stride_axis=0)
        rows.append(jnp.sum(r, axis=0, keepdims=True))
    PFIL[k] = jnp.concatenate(rows, axis=0)


MESH = pl.DeviceIdType.MESH


def remote(src, dst, send, recv, device):
    copy = pltpu.make_async_remote_copy(
        src_ref=src, dst_ref=dst, send_sem=send, recv_sem=recv, device_id=device, device_id_type=MESH
    )
    copy.start()
    return copy


def wait_bytes(ref, sem):
    pltpu.make_async_copy(ref, ref, sem).wait()


def at_coords(x, y, z, c):
    return ((z // 2) * 4 + x, (z % 2) * 8 + y * 2 + c)


def at_chip(p, c):
    return (p // 8, (p % 8) * 2 + c)


def halves(tile, other):
    lane = lax.broadcasted_iota(jnp.int32, tile.shape, 1)
    low = jnp.where(lane < 64, tile, pltpu.roll(other, 64, 1))
    high = jnp.where(lane < 64, pltpu.roll(tile, 64, 1), other)
    return low, high


def split_cores(wide):
    low, high = [], []
    for t in range(4):
        a, b = halves(wide[:, 256 * t:256 * t + 128], wide[:, 256 * t + 128:256 * t + 256])
        low.append(a)
        high.append(b)
    return jnp.concatenate(low, axis=1), jnp.concatenate(high, axis=1)


def exact_dot(value, zero_one, dims=NN):
    first = value.astype(BF16)
    rest = value - first.astype(F32)
    second = rest.astype(BF16)
    third = (rest - second.astype(F32)).astype(BF16)
    return mm(first, zero_one, dims) + mm(second, zero_one, dims) + mm(third, zero_one, dims)


def block_order():
    row = lax.broadcasted_iota(jnp.int32, (512, 512), 0)
    col = lax.broadcasted_iota(jnp.int32, (512, 512), 1)
    goes = ((row // 16) % 4) * 128 + (row // 64) * 16 + row % 16
    return jnp.where(goes == col, 1.0, 0.0).astype(BF16)


def kernel(
    scale,
    strands_hbm, cotangent_hbm, proj_in_hbm, proj_out_hbm, taps_hbm, filters_hbm,
    out_hbm, grad_hbm, gin_hbm, gout_hbm, gshort_hbm, gfil_hbm,
    strands, cotangent, proj_in, proj_out, taps_in, filters_in,
    out_ref, grad_ref, gin_ref, gout_ref, gshort_ref, gfil_ref,
    U, C, W, WO, WSEND, QM, FLIP, TAPS, TF, TB, UT, HID, GP, PART, PSH, PFIL, OUTP, RP,
    SZ, RZ, SXY, RXY, ZH, FS, FIN, GO,
    SMP, SMZ, SMY, SMYR, SMH, SMX,
    in_sem, out_sem, pair_send, pair_recv, halo_send, halo_recv, fwd_send, fwd_recv,
    w_send, w_recv, wo_send, wo_recv,
    z_send, z_recv, xy_send, xy_recv, zh_send, zh_recv, xg_send, xg_recv, go_send, go_recv,
    sm_send, sm_recv, op_send, op_recv,
):
    arrivals = []
    for i, (src, dst) in enumerate((
        (proj_in_hbm, proj_in), (proj_out_hbm, proj_out), (strands_hbm, strands),
        (cotangent_hbm, cotangent), (taps_hbm, taps_in), (filters_hbm, filters_in),
    )):
        copy = pltpu.make_async_copy(src, dst, in_sem.at[i])
        copy.start()
        arrivals.append(copy)
    departures = []

    def leave(i, src, dst):
        copy = pltpu.make_async_copy(src, dst, out_sem.at[i])
        copy.start()
        departures.append(copy)

    seq, ch = lax.axis_index("seq"), lax.axis_index("ch")
    z_hi, x = seq // 4, seq % 4
    z_lo, y, c = ch // 8, (ch // 2) % 4, ch % 2
    z = z_hi * 2 + z_lo
    b = z_lo * 4 + y
    chip = seq * 8 + b
    before, after = (chip + 127) % 128, (chip + 1) % 128
    partner = at_coords(x, y, z, 1 - c)
    z_above, z_below = (z + 1) % 8, (z + 7) % 8
    z_up, z_down = at_coords(x, y, z_above, c), at_coords(x, y, z_below, c)
    is_first = c == 0

    barrier = pltpu.get_barrier_semaphore()
    peers = [partner]
    for zz in (z_above, z_below):
        for cc in (0, 1):
            peers.append(at_coords(x, y, zz, cc))
    for dx in range(4):
        for dy in range(4):
            if dx or dy:
                peers.append(at_coords((x + dx) % 4, (y + dy) % 4, z, c))
    for d in range(1, 4):
        peers.append(at_coords(x, y, (z + 2 * d) % 8, c))
        peers.append(at_coords((x + d) % 4, y, z, 1 - c))
        peers.append(at_coords(x, (y + d) % 4, z, 1 - c))
    for q in (before, after):
        peers.append(at_chip(q, 0))
        peers.append(at_chip(q, 1))
    for peer in peers:
        pl.semaphore_signal(barrier, inc=1, device_id=peer, device_id_type=MESH)

    QM[...] = block_order()
    FLIP[...] = anti_identity(512)
    my_rows = pl.multiple_of(64 * b + 32 * c, 32)
    arrivals[0].wait()
    low, high = [], []
    for s in range(3):
        a, o = split_cores(proj_in[:, pl.ds(s * 1024, 1024)].astype(F32))
        low.append(a)
        high.append(o)
    moved = mm(jnp.concatenate(low + high, axis=0).astype(BF16), QM[...])
    for k in range(4):
        for s in range(3):
            lanes = pl.ds(128 * s, 128)
            even = moved[32 * s:32 * s + 32, 128 * k:128 * k + 128]
            odd = moved[96 + 32 * s:128 + 32 * s, 128 * k:128 * k + 128]
            W[k, pl.ds(my_rows, 32), lanes] = jnp.where(is_first, even, odd).astype(BF16)
            WSEND[k, :, lanes] = jnp.where(is_first, odd, even).astype(BF16)
    arrivals[1].wait()
    for k in range(4):
        WO[k, b] = proj_out[pl.ds(16 * k, 16), :]
    own = pl.multiple_of(144 + 128 * c, 16)
    own_c0 = pl.multiple_of(128 * c, 16)
    arrivals[2].wait()
    U[0, pl.ds(own, 128), :] = strands[0]
    U[1, pl.ds(own, 128), :] = mm(strands[1], FLIP[...]).astype(BF16)
    arrivals[3].wait()
    C[0, pl.ds(own_c0, 128), :] = cotangent[0]
    C[1, pl.ds(own, 128), :] = mm(cotangent[1], FLIP[...]).astype(BF16)
    arrivals[4].wait()
    arrivals[5].wait()
    pl.semaphore_wait(barrier, len(peers))

    def wo_half(m, bb, half):
        return WO.at[m, bb, :, pl.ds(256 * half, 256)]

    def w_half(m, bb, half):
        return W.at[m, pl.ds(pl.multiple_of(64 * bb + 32 * half, 32), 32), :]

    def gather_first(m):
        mine = W.at[m, pl.ds(my_rows, 32), :]
        theirs = WSEND.at[m]
        place = W.at[m, pl.ds(my_rows, 32), :]
        remote(theirs, place, w_send.at[m], w_recv.at[m, 0], partner)
        for d in (1, 3, 2):
            yy = (y + d) % 4
            remote(mine, place, w_send.at[m], w_recv.at[m, 0], at_coords(x, yy, z, c))
            remote(theirs, place, w_send.at[m], w_recv.at[m, 0], at_coords(x, yy, z, 1 - c))
            remote(WO.at[m, b], WO.at[m, b], wo_send.at[m], wo_recv.at[m, 0], at_coords(x, yy, z, c))
        z_side = jnp.where(is_first, z_above, z_below)
        remote(mine, place, w_send.at[m], w_recv.at[m, 1], at_coords(x, y, z_side, c))
        remote(theirs, place, w_send.at[m], w_recv.at[m, 1], at_coords(x, y, z_side, 1 - c))
        for half, side in ((0, z_up), (1, z_down)):
            remote(wo_half(m, b, half), wo_half(m, b, half), wo_send.at[m], wo_recv.at[m, 1], side)

    def gather_second(m):
        wait_bytes(W.at[m, pl.ds(0, 224), :], w_recv.at[m, 0])
        wait_bytes(WO.at[m, pl.ds(0, 3)], wo_recv.at[m, 0])
        for d in (1, 3, 2):
            bb = z_lo * 4 + (y + d) % 4
            for half, side in ((0, z_up), (1, z_down)):
                remote(w_half(m, bb, half), w_half(m, bb, half), w_send.at[m], w_recv.at[m, 1], side)
                remote(wo_half(m, bb, half), wo_half(m, bb, half), wo_send.at[m], wo_recv.at[m, 1], side)

    def gather_last(m):
        wait_bytes(W.at[m, pl.ds(0, 256), :], w_recv.at[m, 1])
        wait_bytes(WO.at[m, pl.ds(0, 4)], wo_recv.at[m, 1])

    def gather_sent(m):
        wait_bytes(W.at[m, pl.ds(0, 480), :], w_send.at[m])
        wait_bytes(WO.at[m, pl.ds(0, 7)], wo_send.at[m])

    gather_first(0)

    far = jnp.where(is_first, before, after)
    near = jnp.where(is_first, after, before)
    big_at = pl.multiple_of(jnp.where(is_first, 400, 16), 16)
    small_src = pl.multiple_of(own + jnp.where(is_first, 112, 0), 16)
    small_at = pl.multiple_of(jnp.where(is_first, 0, 528), 16)
    halo = []
    for s in range(2):
        halo.append(remote(
            U.at[s, pl.ds(own, 128), :], U.at[s, pl.ds(big_at, 128), :],
            halo_send.at[s], halo_recv.at[1 - c], at_chip(far, s)))
        halo.append(remote(
            U.at[s, pl.ds(small_src, 16), :], U.at[s, pl.ds(small_at, 16), :],
            halo_send.at[2 + s], halo_recv.at[2 + c], at_chip(near, s)))
    c_own = pl.multiple_of(jnp.where(is_first, 0, 272), 16)
    c_big = pl.multiple_of(jnp.where(is_first, 256, 16), 16)
    halo.append(remote(
        C.at[c, pl.ds(c_own, 128), :], C.at[c, pl.ds(c_big, 128), :],
        halo_send.at[4], halo_recv.at[4], at_chip(far, c)))
    c_small_src = pl.multiple_of(jnp.where(is_first, 144 + 112, 128), 16)
    c_small = pl.multiple_of(jnp.where(is_first, 0, 384), 16)
    halo.append(remote(
        C.at[1 - c, pl.ds(c_small_src, 16), :], C.at[1 - c, pl.ds(c_small, 16), :],
        halo_send.at[5], halo_recv.at[5], at_chip(near, 1 - c)))
    pair = [
        remote(U.at[s, pl.ds(own, 128), :], U.at[s, pl.ds(own, 128), :], pair_send.at[s], pair_recv.at[s], partner)
        for s in range(2)
    ]
    pair.append(remote(
        C.at[0, pl.ds(own_c0, 128), :], C.at[0, pl.ds(own_c0, 128), :], pair_send.at[2], pair_recv.at[2], partner))
    pair.append(remote(
        C.at[1, pl.ds(own, 128), :], C.at[1, pl.ds(own, 128), :], pair_send.at[3], pair_recv.at[3], partner))
    for m in range(1, 4):
        gather_first(m)

    picked = []
    for s in range(3):
        a, o = split_cores(taps_in[:, pl.ds(s * 1024, 1024)])
        picked.append(jnp.where(is_first, a, o))
    picked = exact_dot(jnp.concatenate(picked, axis=0), QM[...])
    for k in range(4):
        for s in range(3):
            TAPS[k, :, pl.ds(128 * s, 128)] = picked[4 * s:4 * s + 4, 128 * k:128 * k + 128]
    row = lax.broadcasted_iota(jnp.int32, (32, 64), 0)
    col = lax.broadcasted_iota(jnp.int32, (32, 64), 1)
    chosen = jnp.where((row % 8) * 8 + 4 * c + row // 8 == col, 1.0, 0.0).astype(BF16)
    build_tables(mm(chosen, filters_in[...]).astype(BF16), TF, TB)

    gather_second(0)
    wait_bytes(U.at[c, pl.ds(16, 128), :], halo_recv.at[0])
    wait_bytes(U.at[c, pl.ds(400, 128), :], halo_recv.at[1])
    wait_bytes(U.at[c, pl.ds(0, 16), :], halo_recv.at[2])
    wait_bytes(U.at[c, pl.ds(528, 16), :], halo_recv.at[3])
    wait_bytes(C.at[c, pl.ds(c_big, 128), :], halo_recv.at[4])
    wait_bytes(C.at[c, pl.ds(pl.multiple_of(jnp.where(is_first, 384, 0), 16), 16), :], halo_recv.at[5])
    c_halo = pl.multiple_of(jnp.where(is_first, 256, 0), 16)
    c_halo_other = pl.multiple_of(jnp.where(is_first, 0, 256), 16)
    fwd = []
    for i, at in enumerate((0, 400)):
        rows = U.at[c, pl.ds(at, 144), :]
        fwd.append(remote(rows, rows, fwd_send.at[i], fwd_recv.at[i], partner))
    rows = C.at[c, pl.ds(c_halo, 144), :]
    fwd.append(remote(rows, rows, fwd_send.at[2], fwd_recv.at[2], partner))
    for copy in pair:
        copy.wait_recv()
    for s in range(2):
        UT[:, pl.ds(256 * s, 256)] = jnp.transpose(U[s, pl.ds(144, 256), :])
    gather_second(1)
    for i, at in enumerate((0, 400)):
        wait_bytes(U.at[1 - c, pl.ds(at, 144), :], fwd_recv.at[i])
    wait_bytes(C.at[1 - c, pl.ds(c_halo_other, 144), :], fwd_recv.at[2])
    for copy in fwd:
        copy.wait_send()

    @pl.when(chip == 0)
    def _():
        U[:, pl.ds(0, 144), :] = jnp.zeros((2, 144, 512), BF16)
        C[1, pl.ds(0, 144), :] = jnp.zeros((144, 512), BF16)

    @pl.when(chip == 127)
    def _():
        U[:, pl.ds(400, 144), :] = jnp.zeros((2, 144, 512), BF16)
        C[0, pl.ds(256, 144), :] = jnp.zeros((144, 512), BF16)

    def z_start(k):
        SZ[k] = PART[k, pl.ds((1 - z_lo) * 4, 4)].astype(BF16)
        remote(SZ.at[k, :, pl.ds(0, 2)], RZ.at[k, :, pl.ds(0, 2)], z_send.at[k], z_recv.at[k, 0], z_up)
        remote(SZ.at[k, :, pl.ds(2, 2)], RZ.at[k, :, pl.ds(2, 2)], z_send.at[k], z_recv.at[k, 1], z_down)

    def xy_start(k):
        wait_bytes(RZ.at[k, :, pl.ds(0, 2)], z_recv.at[k, 0])
        wait_bytes(RZ.at[k, :, pl.ds(2, 2)], z_recv.at[k, 1])
        SXY[k] = (PART[k, pl.ds(z_lo * 4, 4)] + RZ[k].astype(F32)).astype(BF16)
        for dx in range(4):
            for dy in range(4):
                if dx or dy:
                    xx, yy = (x + dx) % 4, (y + dy) % 4
                    remote(SXY.at[k, yy, xx], RXY.at[k, 4 * dx + dy - 1],
                           xy_send.at[k], xy_recv.at[k], at_coords(xx, yy, z, c))

    def zh_start(k):
        wait_bytes(RXY.at[k], xy_recv.at[k])
        total = SXY[k, y, x].astype(F32)
        for i in range(15):
            total = total + RXY[k, i].astype(F32)
        ZH[k, z_hi] = total.astype(BF16)
        for d in range(1, 4):
            remote(ZH.at[k, z_hi], ZH.at[k, z_hi], zh_send.at[k], zh_recv.at[k], at_coords(x, y, (z + 2 * d) % 8, c))

    target = x // 2
    row_at = pl.multiple_of(16 * (x % 2), 16)
    go_at = pl.multiple_of(128 * x, 128)

    def xg_start(k):
        wait_bytes(ZH.at[k, pl.ds(0, 3)], zh_recv.at[k])
        total = ZH[k, 0].astype(F32)
        for i in range(1, 4):
            total = total + ZH[k, i].astype(F32)
        FS[k] = total.astype(BF16)
        part = FS.at[k, :, pl.ds(0, 384)]
        place = FIN.at[k, c, pl.ds(row_at, 16), :]
        piece = FS.at[k, :, pl.ds(384, 128)]
        spot = GO.at[k, :, pl.ds(go_at, 128)]
        for d in range(1, 4):
            remote(part, place, xg_send.at[k], xg_recv.at[k], at_coords((x + d) % 4, y, z, target))
            remote(piece, spot, go_send.at[k], go_recv.at[k], at_coords((x + d) % 4, y, z, c))

        @pl.when(c == target)
        def _():
            pltpu.make_async_copy(part, place, xg_recv.at[k]).start()

        @pl.when(c != target)
        def _():
            remote(part, place, xg_send.at[k], xg_recv.at[k], partner)

        GO[k, :, pl.ds(go_at, 128)] = FS[k, :, pl.ds(384, 128)]

    def reduced(k):
        wait_bytes(FIN.at[k], xg_recv.at[k])
        wait_bytes(GO.at[k, :, pl.ds(0, 384)], go_recv.at[k])

    def reduce_sent(k):
        wait_bytes(SZ.at[k], z_send.at[k])
        wait_bytes(RXY.at[k], xy_send.at[k])
        wait_bytes(ZH.at[k, pl.ds(0, 3)], zh_send.at[k])
        wait_bytes(FS.at[pl.ds(0, 3), :, pl.ds(0, 384)], xg_send.at[k])
        wait_bytes(FS.at[pl.ds(0, 3), :, pl.ds(384, 128)], go_send.at[k])

        @pl.when(c != target)
        def _():
            wait_bytes(FS.at[k, :, pl.ds(0, 384)], xg_send.at[k])

    def small_z():
        taps_rows = []
        for k in range(4):
            taps_rows.append(jnp.concatenate(
                [PSH[k, :, pl.ds(128 * s, 128)] for s in range(3)], axis=0))
        back = exact_dot(jnp.concatenate(taps_rows, axis=1), QM[...], NT)
        fil = [pltpu.roll(PFIL[k], 255, 1)[:, :128] for k in range(4)]
        for i in range(8):
            m = i // 2
            tiles = (3 * m, 3 * m + 1) if i % 2 == 0 else (3 * m + 1, 3 * m + 2)
            rows = []
            for t in tiles:
                s, p = t // 4, t % 4
                rows.append(back[4 * s:4 * s + 4, 128 * p:128 * p + 128])
            rows += [fil[k][i:i + 1] for k in range(4)]
            SMP[i] = jnp.concatenate(rows + [jnp.zeros((4, 128), F32)], axis=0)
        remote(SMP.at[pl.ds((1 - z_lo) * 4, 4)], SMZ, sm_send.at[0], sm_recv.at[0], z_up)

    def small_y():
        wait_bytes(SMZ, sm_recv.at[0])
        SMY[...] = SMP[pl.ds(z_lo * 4, 4)] + SMZ[...]
        for d in range(1, 4):
            yy = (y + d) % 4
            remote(SMY.at[yy], SMYR.at[d - 1], sm_send.at[1], sm_recv.at[1], at_coords(x, yy, z, c))

    def small_h():
        wait_bytes(SMYR, sm_recv.at[1])
        SMH[z_hi] = SMY[y] + SMYR[0] + SMYR[1] + SMYR[2]
        for d in range(1, 4):
            remote(SMH.at[z_hi], SMH.at[z_hi], sm_send.at[2], sm_recv.at[2], at_coords(x, y, (z + 2 * d) % 8, c))

    def small_x():
        wait_bytes(SMH.at[pl.ds(0, 3)], sm_recv.at[2])
        SMX[c, x] = SMH[0] + SMH[1] + SMH[2] + SMH[3]
        for d in range(1, 4):
            for cc in (c, 1 - c):
                remote(SMX.at[c, x], SMX.at[c, x], sm_send.at[3], sm_recv.at[3], at_coords((x + d) % 4, y, z, cc))
        remote(SMX.at[c, x], SMX.at[c, x], sm_send.at[3], sm_recv.at[3], partner)

    def small_last():
        wait_bytes(SMP.at[pl.ds(0, 7)], sm_recv.at[3])
        e = SMX[0, 0] + SMX[0, 1] + SMX[0, 2] + SMX[0, 3]
        o = SMX[1, 0] + SMX[1, 1] + SMX[1, 2] + SMX[1, 3]
        mine = jnp.where(is_first, e, o)
        gfil_ref[...] = exact_dot(mine, anti_identity(128))[8:12] * scale
        lane = lax.broadcasted_iota(jnp.int32, (4, 128), 1)

        def blocks(v):
            a, t = v[0:4], v[4:8]
            turned_a, turned_t = pltpu.roll(a, 64, 1), pltpu.roll(t, 64, 1)
            even = b % 2 == 0
            return (
                jnp.where(even, a, turned_a),
                jnp.where(even, turned_a, t),
                jnp.where(even, t, turned_t),
            )

        e, o = blocks(e), blocks(o)
        one = jnp.where(is_first, e[0], o[1])
        two = jnp.where(is_first, o[0], e[2])
        three = jnp.where(is_first, e[1], o[2])
        gshort_ref[:, pl.ds(0, 128)] = jnp.where(lane < 64, one, pltpu.roll(two, 64, 1)) * scale
        gshort_ref[:, pl.ds(128, 64)] = three[:, :64] * scale

    def small_sent():
        wait_bytes(SMZ, sm_send.at[0])
        wait_bytes(SMYR, sm_send.at[1])
        wait_bytes(SMYR, sm_send.at[2])
        wait_bytes(SMP.at[pl.ds(0, 7)], sm_send.at[3])


    def body(k, carry):
        gather_last(k)

        def hook_a():
            @pl.when(k == 0)
            def _():
                gather_second(2)

        def hook_b():
            @pl.when(k == 0)
            def _():
                gather_second(3)

        compute_chunk(k, U, C, W, WO, TAPS, TF, TB, UT, HID, GP, PART, PSH, PFIL, hook_a, hook_b)
        z_start(k)

        @pl.when(k >= 1)
        def _():
            xy_start(k - 1)

        @pl.when(k >= 2)
        def _():
            zh_start(k - 2)

        @pl.when(k >= 3)
        def _():
            xg_start(k - 3)

        return carry

    lax.fori_loop(0, 4, body, 0)

    small_z()
    other_rows = 128 * (1 - c)
    op = []
    for o in range(2):
        if o == 0:
            res = mm(HID[0], WO[0].reshape(128, 512))
            for k in range(1, 4):
                res = res + mm(HID[k], WO[k].reshape(128, 512))
        else:
            res = mm(GP[0], W[0], NT)
            for k in range(1, 4):
                res = res + mm(GP[k], W[k], NT)
        OUTP[o] = res
        for s in range(2):
            rows = pl.ds(pl.multiple_of(256 * s + other_rows, 128), 128)
            op.append(remote(OUTP.at[o, rows, :], RP.at[o, s], op_send.at[o, s], op_recv.at[o, s], partner))
    xy_start(3)
    small_y()
    for o, (ref, hbm) in enumerate(((out_ref, out_hbm), (grad_ref, grad_hbm))):
        for s in range(2):
            op[2 * o + s].wait_recv()
            rows = pl.ds(pl.multiple_of(256 * s + 128 * c, 128), 128)
            value = (OUTP[o, rows, :] + RP[o, s]).astype(BF16)
            ref[s] = value if s == 0 else mm(value, FLIP[...]).astype(BF16)
        leave(o, ref, hbm)
    zh_start(2)
    xg_start(1)
    small_h()
    zh_start(3)
    xg_start(2)
    small_x()
    xg_start(3)
    for copy in pair + halo + op:
        copy.wait_send()
    for m in range(4):
        gather_sent(m)
    small_last()
    leave(4, gshort_ref, gshort_hbm)
    leave(5, gfil_ref, gfil_hbm)
    for k in range(4):
        reduced(k)
    for k in range(4):
        gout_ref[pl.ds(16 * k, 16), :] = GO[k].astype(F32) * scale
    leave(3, gout_ref, gout_hbm)
    rows = []
    for cc in range(2):
        for s in range(3):
            rows.append(jnp.concatenate([FIN[k, cc, :, pl.ds(128 * s, 128)] for k in range(4)], axis=1))
    back = mm(jnp.concatenate(rows, axis=0), QM[...], NT) * scale
    for s in range(3):
        for t in range(4):
            lanes = slice(128 * t, 128 * t + 128)
            first, second = halves(back[32 * s:32 * s + 32, lanes], back[96 + 32 * s:128 + 32 * s, lanes])
            gin_ref[:, pl.ds(s * 1024 + t * 256, 128)] = first
            gin_ref[:, pl.ds(s * 1024 + t * 256 + 128, 128)] = second
    leave(2, gin_ref, gin_hbm)
    for k in range(4):
        reduce_sent(k)
    small_sent()
    for copy in departures:
        copy.wait()


def hand_over(*refs):
    n = 6
    sources, targets, held = refs[:n], refs[n:2 * n], refs[2 * n:3 * n]
    in_sem, out_sem = refs[3 * n:]
    arrive = [pltpu.make_async_copy(sources[i], held[i], in_sem.at[i]) for i in range(n)]
    leave = [pltpu.make_async_copy(held[i], targets[i], out_sem.at[i]) for i in range(n)]
    for copy in arrive:
        copy.start()
    for i in range(n):
        arrive[i].wait()
        leave[i].start()
    for copy in leave:
        copy.wait()


def shards(strands, cotangent, proj_in, proj_out, short_taps, filters):
    length = strands.shape[1] * lax.axis_size(("seq", "ch"))
    scale = float(length) ** (-0.5)
    dma = pltpu.SemaphoreType.DMA
    outs = (
        jax.ShapeDtypeStruct((2, 128, 512), BF16),
        jax.ShapeDtypeStruct((2, 128, 512), BF16),
        jax.ShapeDtypeStruct((32, 3072), F32),
        jax.ShapeDtypeStruct((64, 512), F32),
        jax.ShapeDtypeStruct((4, 192), F32),
        jax.ShapeDtypeStruct((4, 128), F32),
    )
    scratch = [
        pltpu.VMEM((2, 128, 512), BF16),
        pltpu.VMEM((2, 128, 512), BF16),
        pltpu.VMEM((32, 3072), BF16),
        pltpu.VMEM((64, 512), BF16),
        pltpu.VMEM((4, 3072), F32),
        pltpu.VMEM((64, 128), BF16),
    ]
    scratch += [pltpu.VMEM(o.shape, o.dtype) for o in outs]
    scratch += [
        pltpu.VMEM((2, 544, 512), BF16),
        pltpu.VMEM((2, 400, 512), BF16),
        pltpu.VMEM((4, 512, 384), BF16),
        pltpu.VMEM((4, 8, 16, 512), BF16),
        pltpu.VMEM((4, 32, 384), BF16),
        pltpu.VMEM((512, 512), BF16),
        pltpu.VMEM((512, 512), BF16),
        pltpu.VMEM((4, 4, 384), F32),
        pltpu.VMEM((4, 1024, 256), BF16),
        pltpu.VMEM((4, 1024, 256), BF16),
        pltpu.VMEM((512, 512), BF16),
        pltpu.VMEM((4, 512, 128), BF16),
        pltpu.VMEM((4, 512, 384), BF16),
        pltpu.VMEM((4, 8, 4, 16, 512), F32),
        pltpu.VMEM((4, 4, 384), F32),
        pltpu.VMEM((4, 8, 256), F32),
        pltpu.VMEM((2, 512, 512), F32),
        pltpu.VMEM((2, 2, 128, 512), F32),
        pltpu.VMEM((4, 4, 4, 16, 512), BF16),
        pltpu.VMEM((4, 4, 4, 16, 512), BF16),
        pltpu.VMEM((4, 4, 4, 16, 512), BF16),
        pltpu.VMEM((4, 15, 16, 512), BF16),
        pltpu.VMEM((4, 4, 16, 512), BF16),
        pltpu.VMEM((4, 16, 512), BF16),
        pltpu.VMEM((4, 2, 32, 384), BF16),
        pltpu.VMEM((4, 16, 512), BF16),
        pltpu.VMEM((8, 16, 128), F32),
        pltpu.VMEM((4, 16, 128), F32),
        pltpu.VMEM((4, 16, 128), F32),
        pltpu.VMEM((3, 16, 128), F32),
        pltpu.VMEM((4, 16, 128), F32),
        pltpu.VMEM((2, 4, 16, 128), F32),
    ]
    scratch += [
        dma((6,)), dma((6,)), dma((4,)), dma((4,)), dma((6,)), dma((6,)), dma((3,)), dma((3,)),
        dma((4,)), dma((4, 2)), dma((4,)), dma((4, 2)),
        dma((4,)), dma((4, 2)), dma((4,)), dma((4,)), dma((4,)), dma((4,)), dma((4,)), dma((4,)), dma((4,)), dma((4,)),
        dma((4,)), dma((4,)), dma((2, 2)), dma((2, 2)),
    ]
    anywhere = pl.BlockSpec(memory_space=pl.ANY)
    results = pl.pallas_call(
        functools.partial(kernel, scale),
        out_shape=outs,
        in_specs=[anywhere] * 6,
        out_specs=tuple([anywhere] * 6),
        scratch_shapes=scratch,
        compiler_params=pltpu.CompilerParams(
            collective_id=0, has_side_effects=True, vmem_limit_bytes=58 * 2**20
        ),
        cost_estimate=pl.CostEstimate(flops=9 * 10**9, bytes_accessed=4 * 10**6, transcendentals=0),
    )(strands, cotangent, proj_in, proj_out, short_taps.T, filters)
    results = pl.pallas_call(
        hand_over,
        out_shape=outs,
        in_specs=[anywhere] * 6,
        out_specs=tuple([anywhere] * 6),
        scratch_shapes=[pltpu.VMEM(o.shape, o.dtype) for o in outs] + [dma((6,)), dma((6,))],
    )(*results)
    return results[:4] + (results[4].T, results[5])


def solution(mesh):
    placed = P(None, ("seq", "ch"), None)
    rows = P("ch", None)
    return jax.shard_map(
        shards,
        mesh=mesh,
        in_specs=(placed, placed, rows, rows, P(), P()),
        out_specs=(placed, placed, rows, rows, rows, rows),
        check_vma=False,
    )
```

time: 83 us -> 72.8 us (0.88)
  the two profiles are of different devices: /device:TPU:8 before, /device:TPU:1 now
where the time goes in v2:
time: 72.8 us; the launch traced here: 72.6 us
  Pallas kernels  72 us (99%)
    pallas_call x1, Pallas kernels, shards(): pl.pallas_call(functools.partial(kernel, scale), out_shape=outs, in_specs...  70 us
    pallas_call x1, Pallas kernels, shards(): pl.pallas_call(hand_over, out_shape=outs, in_specs=[anywhere] * 6, out_sp...  2.05 us

profile of v2, /device:TPU:1, one launch (start us, length us, event | category | flops | bytes accessed | tf_op | source)
XLA Modules:
  0.0 72.6 jit_solution(12729420710423573615)
XLA Ops:
  0.6 70.0 %shard_map.109 = (bf16[2,128,512]{2,1,0:T(8,128)(2,1)}, bf16[2,128,512]{2,1,0:T(8,128)(2,1)}, f32[32,3072]{1,0:T(8,128)}, f32[64,512]{1,0:T(8,128)}, f32[4,192]{1,0:T(4,128)}, /*index=5*/f32[4,128]{1,0:T(4,128)}) custom-call(bf16[2,128,512]{2,1,0:T(8,128)(2,1)} %strands_hbm.1, bf16[2,128,512]{2,1,0:T(8,128)(2,1)} %cotangent_hbm.1, ...), custom_call_target="tpu_custom_call" | custom-call | flops 8999999488 | bytes 4000000 | tf_op jit(solution)/shard_map/pallas_call | solution.py:744
  70.6 2.0 %shard_map.110 = (bf16[2,128,512]{2,1,0:T(8,128)(2,1)}, bf16[2,128,512]{2,1,0:T(8,128)(2,1)}, f32[32,3072]{1,0:T(8,128)}, f32[64,512]{1,0:T(8,128)}, f32[4,192]{1,0:T(4,128)}, /*index=5*/f32[4,128]{1,0:T(4,128)}) custom-call(bf16[2,128,512]{2,1,0:T(8,128)(2,1)} %get-tuple-element.18.refs_0_, bf16[2,128,512]{2,1,0:T(8,128)(2,1)} %get-tuple-element.19.refs_1_, ...), custom_call_target="tpu_custom_call" | custom-call | tf_op jit(solution)/shard_map/pallas_call | solution.py:755

commit v3 on v2

--- a/solution.py
+++ b/solution.py
@@ -18,8 +18,15 @@
     return lax.dot_general(a, b, dims, preferred_element_type=F32)
 
 
-def lane_group(shape):
-    return (lax.broadcasted_iota(jnp.int32, shape, 1) % 128) // 16
+def lane_group(shape, span):
+    return (lax.broadcasted_iota(jnp.int32, shape, 1) % span) // 16
+
+
+def halves(tile, other):
+    lane = lax.broadcasted_iota(jnp.int32, tile.shape, 1)
+    low = jnp.where(lane < 64, tile, pltpu.roll(other, 64, 1))
+    high = jnp.where(lane < 64, pltpu.roll(tile, 64, 1), other)
+    return low, high
 
 
 def build_tables(filters, TF, TB):
@@ -42,27 +49,21 @@
     return jnp.where(r + c == n - 1, 1.0, 0.0).astype(BF16)
 
 
-def diag(products, rows):
-    group = lane_group((rows, products.shape[1]))
+def diag(products, rows, count):
+    group = lane_group((rows, products.shape[1]), 16 * count)
     out = products[0:rows]
-    for g in range(1, 8):
+    for g in range(1, count):
         out = jnp.where(group == g, products[g * rows:(g + 1) * rows], out)
     return out
 
 
-def shifted(x, j):
-    if j == 0:
-        return x
-    return pltpu.roll(x, j % x.shape[0], 0)
-
-
-def compute_chunk(k, U, C, Win, Wout, taps_ref, TF, TB, UT, HID, GP, PART, PSH, PFIL, hook_a, hook_b):
+def compute_chunk(k, U, C, Win, Wout, taps_ref, TF, TB, UT, HID, GP, PART, PSH, PFIL, ROWS, hook_a, hook_b):
     w = Win[k]
     wo = Wout[k].reshape(128, 512)
     taps = taps_ref[k]
     tf = TF[k]
     tb = TB[k]
-    proj, gated, gc, keys, values, queries, ghs = [], [], [], [], [], [], []
+    own_proj, gated, gc, keys, values, queries, ghs = [], [], [], [], [], [], []
     for s in range(2):
         sign = 1 if s == 0 else -1
         kv_at = 0 if s == 0 else 128
@@ -70,14 +71,20 @@
         pkv = mm(U[s, pl.ds(kv_at, 416), :], w[:, 128:]).astype(BF16)
         pq = mm(U[s, pl.ds(q_at, 416), :], w[:, :128]).astype(BF16)
         gh = mm(C[s], wo, NT).astype(BF16).astype(F32)
-        pkv32 = pkv.astype(F32)
-        pq32 = pq.astype(F32)
-        mkv = jnp.zeros((416, 256), F32)
-        mq = jnp.zeros((416, 128), F32)
-        for j in range(4):
-            mkv = mkv + taps[j:j + 1, 128:] * shifted(pkv32, sign * j)
-            mq = mq + taps[j:j + 1, :128] * shifted(pq32, sign * j)
-        key, value = mkv[:, :128], mkv[:, 128:]
+        mixed = []
+        own_kv = 144 if s == 0 else 16
+        own_q = 160 - own_kv
+        for part, values_in in enumerate((pq, pkv[:, :128], pkv[:, 128:])):
+            held = ROWS.at[3 * s + part]
+            wide = values_in.astype(F32)
+            held[pl.ds(8, 416), :] = wide
+            t = taps[:, 128 * part:128 * part + 128]
+            total = t[0:1] * wide
+            for j in range(1, 4):
+                total = total + t[j:j + 1] * held[pl.ds(8 - sign * j, 416), :]
+            mixed.append(total)
+        mq, key, value = mixed
+        own_proj.append((own_q, own_kv, own_kv))
         gated.append((key * value).astype(BF16))
         keys.append(key)
         values.append(value)
@@ -85,44 +92,54 @@
         ghs.append(gh)
         at = 16 if s == 0 else 0
         gc.append((gh * mq[at:at + 400]).astype(BF16))
-        own_kv = 144 if s == 0 else 16
-        own_q = 160 - own_kv
-        proj.append((pq32[own_q:own_q + 256], pkv32[own_kv:own_kv + 256]))
     hook_a()
-    wf = jnp.concatenate([gated[0][:400], gc[1]], axis=1)
-    f_parts, b_parts = [], []
-    prods = None
-    for blk in range(2):
-        xf = wf[16 + 128 * blk:272 + 128 * blk]
-        f_parts.append(diag(mm(tf, xf), 128))
-        xb = jnp.concatenate([gc[0][128 * blk:128 * blk + 256], gated[1][16 + 128 * blk:272 + 128 * blk]], axis=1)
-        b_parts.append(diag(mm(tb, xb), 128))
-        left = jnp.concatenate([gc[0][128 * blk:128 * blk + 128], gated[1][16 + 128 * blk:144 + 128 * blk]], axis=1)
-        left = mm(anti_identity(128), left).astype(BF16)
-        group = lane_group((128, 256))
-        masked = jnp.concatenate([jnp.where(group == g, left, jnp.zeros_like(left)) for g in range(8)], axis=0)
-        term = mm(masked, xf, NT)
-        prods = term if prods is None else prods + term
+    def packed(first, second):
+        low_first, high_first = halves(*first)
+        low_second, high_second = halves(*second)
+        return (
+            jnp.concatenate([low_first, low_second], axis=1),
+            jnp.concatenate([high_first, high_second], axis=1),
+        )
+
+    def blocks_of(value, at, rows):
+        return value[at:at + rows], value[at + 128:at + 128 + rows]
+
+    xf = packed(blocks_of(gated[0], 16, 256), blocks_of(gc[1], 16, 256))
+    xb = packed(blocks_of(gc[0], 0, 256), blocks_of(gated[1], 16, 256))
+    left = packed(blocks_of(gc[0], 0, 128), blocks_of(gated[1], 16, 128))
+    reverse = anti_identity(128)
+    group = lane_group((128, 256), 64)
+    yf, yb, prods = [], [], []
+    for h in range(2):
+        yf.append(diag(mm(tf[512 * h:512 * h + 512], xf[h]), 128, 4))
+        yb.append(diag(mm(tb[512 * h:512 * h + 512], xb[h]), 128, 4))
+        turned = mm(reverse, left[h]).astype(BF16)
+        masked = jnp.concatenate([jnp.where(group == g, turned, jnp.zeros_like(turned)) for g in range(4)], axis=0)
+        prods.append(mm(masked, xf[h], NT))
+    f_first_strand = halves(yf[0][:, :128], yf[1][:, :128])
+    f_second_strand = halves(yf[0][:, 128:], yf[1][:, 128:])
+    b_first_strand = halves(yb[0][:, :128], yb[1][:, :128])
+    b_second_strand = halves(yb[0][:, 128:], yb[1][:, 128:])
     tf3 = tf.reshape(8, 128, 256)
     tb3 = tb.reshape(8, 128, 256)
     f_last = tf3[:, 112:].reshape(128, 256)
     f_first = tf3[:, :16].reshape(128, 256)
     b_last = tb3[:, 112:].reshape(128, 256)
     b_first = tb3[:, :16].reshape(128, 256)
-    conv0_x = diag(mm(f_last, gated[0][160:416]), 16)
-    gg1_x = diag(mm(f_first, gc[1][0:256]), 16)
-    gg0_x = diag(mm(b_last, gc[0][144:400]), 16)
-    conv1_x = diag(mm(b_first, gated[1][0:256]), 16)
+    conv0_x = diag(mm(f_last, gated[0][160:416]), 16, 8)
+    gg1_x = diag(mm(f_first, gc[1][0:256]), 16, 8)
+    gg0_x = diag(mm(b_last, gc[0][144:400]), 16, 8)
+    conv1_x = diag(mm(b_first, gated[1][0:256]), 16, 8)
     conv = [
-        jnp.concatenate([f_parts[0][:, :128], f_parts[1][:, :128], conv0_x], axis=0),
-        jnp.concatenate([conv1_x, b_parts[0][:, 128:], b_parts[1][:, 128:]], axis=0),
+        jnp.concatenate([*f_first_strand, conv0_x], axis=0),
+        jnp.concatenate([conv1_x, *b_second_strand], axis=0),
     ]
     gg = [
-        jnp.concatenate([b_parts[0][:, :128], b_parts[1][:, :128], gg0_x], axis=0),
-        jnp.concatenate([gg1_x, f_parts[0][:, 128:], f_parts[1][:, 128:]], axis=0),
+        jnp.concatenate([*b_first_strand, gg0_x], axis=0),
+        jnp.concatenate([gg1_x, *f_second_strand], axis=0),
     ]
     hook_b()
-    short = [jnp.zeros((1, 384), F32) for _ in range(4)]
+    short = [[None] * 3 for _ in range(4)]
     for s in range(2):
         sign = 1 if s == 0 else -1
         own = 0 if s == 0 else 16
@@ -132,22 +149,28 @@
         query = queries[s][q_at:q_at + 272]
         hidden = (query[own:own + 256] * conv[s][own:own + 256]).astype(BF16)
         HID[k, pl.ds(256 * s, 256), :] = hidden
-        gm = jnp.concatenate(
-            [
-                ghs[s][gh_at:gh_at + 272] * conv[s],
-                gg[s] * values[s][kv_at:kv_at + 272],
-                gg[s] * keys[s][kv_at:kv_at + 272],
-            ],
-            axis=1,
-        ).astype(BF16).astype(F32)
-        p_own = jnp.concatenate(proj[s], axis=1)
-        total = jnp.zeros((256, 384), F32)
-        for j in range(4):
-            moved = shifted(gm, -sign * j)[own:own + 256]
-            total = total + taps[j:j + 1] * moved
-            short[j] = short[j] + jnp.sum(p_own * moved, axis=0, keepdims=True)
-        GP[k, pl.ds(256 * s, 256), :] = total.astype(BF16)
-    PSH[k] = jnp.concatenate(short, axis=0)
+        grads = (
+            ghs[s][gh_at:gh_at + 272] * conv[s],
+            gg[s] * values[s][kv_at:kv_at + 272],
+            gg[s] * keys[s][kv_at:kv_at + 272],
+        )
+        for part in range(3):
+            held = ROWS.at[6 + 3 * s + part]
+            p_own = ROWS[3 * s + part, pl.ds(8 + own_proj[s][part], 256), :]
+            gm = grads[part].astype(BF16).astype(F32)
+            held[pl.ds(8, 272), :] = gm
+            t = taps[:, 128 * part:128 * part + 128]
+            total = None
+            for j in range(4):
+                moved = gm[own:own + 256] if j == 0 else held[pl.ds(8 + own + sign * j, 256), :]
+                term = t[j:j + 1] * moved
+                total = term if total is None else total + term
+                column = jnp.sum(p_own * moved, axis=0, keepdims=True)
+                short[j][part] = column if s == 0 else short[j][part] + column
+            GP[k, pl.ds(256 * s, 256), pl.ds(128 * part, 128)] = total.astype(BF16)
+    for j in range(4):
+        for part in range(3):
+            PSH[k, pl.ds(j, 1), pl.ds(128 * part, 128)] = short[j][part]
     PART[k, :, :, :, pl.ds(0, 384)] = mm(UT[...], GP[k]).reshape(8, 4, 16, 384)
     po = mm(HID[k, pl.ds(0, 256), :], C[0, pl.ds(0, 256), :], TN)
     po = po + mm(HID[k, pl.ds(256, 256), :], C[1, pl.ds(144, 256), :], TN)
@@ -155,7 +178,7 @@
         PART[k, :, q, :, pl.ds(384, 128)] = po[:, 128 * q:128 * q + 128].reshape(8, 16, 128)
     rows = []
     for g in range(8):
-        r = pltpu.roll(prods[128 * g:128 * g + 128], 129, 1, stride=1, stride_axis=0)
+        r = pltpu.roll(prods[g // 4][128 * (g % 4):128 * (g % 4) + 128], 129, 1, stride=1, stride_axis=0)
         rows.append(jnp.sum(r, axis=0, keepdims=True))
     PFIL[k] = jnp.concatenate(rows, axis=0)
 
@@ -181,13 +204,6 @@
 
 def at_chip(p, c):
     return (p // 8, (p % 8) * 2 + c)
-
-
-def halves(tile, other):
-    lane = lax.broadcasted_iota(jnp.int32, tile.shape, 1)
-    low = jnp.where(lane < 64, tile, pltpu.roll(other, 64, 1))
-    high = jnp.where(lane < 64, pltpu.roll(tile, 64, 1), other)
-    return low, high
 
 
 def split_cores(wide):
@@ -220,7 +236,7 @@
     out_hbm, grad_hbm, gin_hbm, gout_hbm, gshort_hbm, gfil_hbm,
     strands, cotangent, proj_in, proj_out, taps_in, filters_in,
     out_ref, grad_ref, gin_ref, gout_ref, gshort_ref, gfil_ref,
-    U, C, W, WO, WSEND, QM, FLIP, TAPS, TF, TB, UT, HID, GP, PART, PSH, PFIL, OUTP, RP,
+    U, C, W, WO, WSEND, QM, FLIP, TAPS, TF, TB, UT, HID, GP, PART, PSH, PFIL, ROWS, OUTP, RP,
     SZ, RZ, SXY, RXY, ZH, FS, FIN, GO,
     SMP, SMZ, SMY, SMYR, SMH, SMX,
     in_sem, out_sem, pair_send, pair_recv, halo_send, halo_recv, fwd_send, fwd_recv,
@@ -582,20 +598,12 @@
             def _():
                 gather_second(3)
 
-        compute_chunk(k, U, C, W, WO, TAPS, TF, TB, UT, HID, GP, PART, PSH, PFIL, hook_a, hook_b)
+        compute_chunk(k, U, C, W, WO, TAPS, TF, TB, UT, HID, GP, PART, PSH, PFIL, ROWS, hook_a, hook_b)
         z_start(k)
-
-        @pl.when(k >= 1)
-        def _():
-            xy_start(k - 1)
 
         @pl.when(k >= 2)
         def _():
-            zh_start(k - 2)
-
-        @pl.when(k >= 3)
-        def _():
-            xg_start(k - 3)
+            xy_start(k - 2)
 
         return carry
 
@@ -609,6 +617,7 @@
             res = mm(HID[0], WO[0].reshape(128, 512))
             for k in range(1, 4):
                 res = res + mm(HID[k], WO[k].reshape(128, 512))
+            xy_start(2)
         else:
             res = mm(GP[0], W[0], NT)
             for k in range(1, 4):
@@ -617,6 +626,7 @@
         for s in range(2):
             rows = pl.ds(pl.multiple_of(256 * s + other_rows, 128), 128)
             op.append(remote(OUTP.at[o, rows, :], RP.at[o, s], op_send.at[o, s], op_recv.at[o, s], partner))
+    zh_start(0)
     xy_start(3)
     small_y()
     for o, (ref, hbm) in enumerate(((out_ref, out_hbm), (grad_ref, grad_hbm))):
@@ -626,12 +636,14 @@
             value = (OUTP[o, rows, :] + RP[o, s]).astype(BF16)
             ref[s] = value if s == 0 else mm(value, FLIP[...]).astype(BF16)
         leave(o, ref, hbm)
+    zh_start(1)
+    xg_start(0)
+    small_h()
     zh_start(2)
     xg_start(1)
-    small_h()
     zh_start(3)
+    small_x()
     xg_start(2)
-    small_x()
     xg_start(3)
     for copy in pair + halo + op:
         copy.wait_send()
@@ -717,6 +729,7 @@
         pltpu.VMEM((4, 8, 4, 16, 512), F32),
         pltpu.VMEM((4, 4, 384), F32),
         pltpu.VMEM((4, 8, 256), F32),
+        pltpu.VMEM((12, 432, 128), F32),
         pltpu.VMEM((2, 512, 512), F32),
         pltpu.VMEM((2, 2, 128, 512), F32),
         pltpu.VMEM((4, 4, 4, 16, 512), BF16),

time: 72.8 us -> 68 us (0.934)
  Pallas kernels: 72 us -> 67.2 us
    pallas_call x1, Pallas kernels: 70 us -> 65.2 us  [shards(): pl.pallas_call(functools.partial(kernel, scale), out_shape=outs, in_specs...]
where the time goes in v3:
time: 68 us; the launch traced here: 67.8 us
  Pallas kernels  67.2 us (99%)
    pallas_call x1, Pallas kernels, shards(): pl.pallas_call(functools.partial(kernel, scale), out_shape=outs, in_specs...  65.2 us
    pallas_call x1, Pallas kernels, shards(): pl.pallas_call(hand_over, out_shape=outs, in_specs=[anywhere] * 6, out_sp...  2.05 us

profile of v3, /device:TPU:1, one launch (start us, length us, event | category | flops | bytes accessed | tf_op | source)
XLA Modules:
  0.0 67.8 jit_solution(4844322961776735670)
XLA Ops:
  0.6 65.2 %shard_map.109 = (bf16[2,128,512]{2,1,0:T(8,128)(2,1)}, bf16[2,128,512]{2,1,0:T(8,128)(2,1)}, f32[32,3072]{1,0:T(8,128)}, f32[64,512]{1,0:T(8,128)}, f32[4,192]{1,0:T(4,128)}, /*index=5*/f32[4,128]{1,0:T(4,128)}) custom-call(bf16[2,128,512]{2,1,0:T(8,128)(2,1)} %strands_hbm.1, bf16[2,128,512]{2,1,0:T(8,128)(2,1)} %cotangent_hbm.1, ...), custom_call_target="tpu_custom_call" | custom-call | flops 8999999488 | bytes 4000000 | tf_op jit(solution)/shard_map/pallas_call | solution.py:757
  65.8 2.0 %shard_map.110 = (bf16[2,128,512]{2,1,0:T(8,128)(2,1)}, bf16[2,128,512]{2,1,0:T(8,128)(2,1)}, f32[32,3072]{1,0:T(8,128)}, f32[64,512]{1,0:T(8,128)}, f32[4,192]{1,0:T(4,128)}, /*index=5*/f32[4,128]{1,0:T(4,128)}) custom-call(bf16[2,128,512]{2,1,0:T(8,128)(2,1)} %get-tuple-element.18.refs_0_, bf16[2,128,512]{2,1,0:T(8,128)(2,1)} %get-tuple-element.19.refs_1_, ...), custom_call_target="tpu_custom_call" | custom-call | tf_op jit(solution)/shard_map/pallas_call | solution.py:768

commit v4 on v3

--- a/solution.py
+++ b/solution.py
@@ -233,13 +233,12 @@
 def kernel(
     scale,
     strands_hbm, cotangent_hbm, proj_in_hbm, proj_out_hbm, taps_hbm, filters_hbm,
-    out_hbm, grad_hbm, gin_hbm, gout_hbm, gshort_hbm, gfil_hbm,
+    out_ref, grad_ref, gin_ref, gout_ref, gshort_ref, gfil_ref,
     strands, cotangent, proj_in, proj_out, taps_in, filters_in,
-    out_ref, grad_ref, gin_ref, gout_ref, gshort_ref, gfil_ref,
     U, C, W, WO, WSEND, QM, FLIP, TAPS, TF, TB, UT, HID, GP, PART, PSH, PFIL, ROWS, OUTP, RP,
     SZ, RZ, SXY, RXY, ZH, FS, FIN, GO,
     SMP, SMZ, SMY, SMYR, SMH, SMX,
-    in_sem, out_sem, pair_send, pair_recv, halo_send, halo_recv, fwd_send, fwd_recv,
+    in_sem, pair_send, pair_recv, halo_send, halo_recv, fwd_send, fwd_recv,
     w_send, w_recv, wo_send, wo_recv,
     z_send, z_recv, xy_send, xy_recv, zh_send, zh_recv, xg_send, xg_recv, go_send, go_recv,
     sm_send, sm_recv, op_send, op_recv,
@@ -252,13 +251,6 @@
         copy = pltpu.make_async_copy(src, dst, in_sem.at[i])
         copy.start()
         arrivals.append(copy)
-    departures = []
-
-    def leave(i, src, dst):
-        copy = pltpu.make_async_copy(src, dst, out_sem.at[i])
-        copy.start()
-        departures.append(copy)
-
     seq, ch = lax.axis_index("seq"), lax.axis_index("ch")
     z_hi, x = seq // 4, seq % 4
     z_lo, y, c = ch // 8, (ch // 2) % 4, ch % 2
@@ -335,9 +327,10 @@
         remote(theirs, place, w_send.at[m], w_recv.at[m, 0], partner)
         for d in (1, 3, 2):
             yy = (y + d) % 4
-            remote(mine, place, w_send.at[m], w_recv.at[m, 0], at_coords(x, yy, z, c))
-            remote(theirs, place, w_send.at[m], w_recv.at[m, 0], at_coords(x, yy, z, 1 - c))
-            remote(WO.at[m, b], WO.at[m, b], wo_send.at[m], wo_recv.at[m, 0], at_coords(x, yy, z, c))
+            kind = 2 if d == 2 else 0
+            remote(mine, place, w_send.at[m], w_recv.at[m, kind], at_coords(x, yy, z, c))
+            remote(theirs, place, w_send.at[m], w_recv.at[m, kind], at_coords(x, yy, z, 1 - c))
+            remote(WO.at[m, b], WO.at[m, b], wo_send.at[m], wo_recv.at[m, kind], at_coords(x, yy, z, c))
         z_side = jnp.where(is_first, z_above, z_below)
         remote(mine, place, w_send.at[m], w_recv.at[m, 1], at_coords(x, y, z_side, c))
         remote(theirs, place, w_send.at[m], w_recv.at[m, 1], at_coords(x, y, z_side, 1 - c))
@@ -345,9 +338,12 @@
             remote(wo_half(m, b, half), wo_half(m, b, half), wo_send.at[m], wo_recv.at[m, 1], side)
 
     def gather_second(m):
-        wait_bytes(W.at[m, pl.ds(0, 224), :], w_recv.at[m, 0])
-        wait_bytes(WO.at[m, pl.ds(0, 3)], wo_recv.at[m, 0])
+        wait_bytes(W.at[m, pl.ds(0, 160), :], w_recv.at[m, 0])
+        wait_bytes(WO.at[m, pl.ds(0, 2)], wo_recv.at[m, 0])
         for d in (1, 3, 2):
+            if d == 2:
+                wait_bytes(W.at[m, pl.ds(0, 64), :], w_recv.at[m, 2])
+                wait_bytes(WO.at[m, 0], wo_recv.at[m, 2])
             bb = z_lo * 4 + (y + d) % 4
             for half, side in ((0, z_up), (1, z_down)):
                 remote(w_half(m, bb, half), w_half(m, bb, half), w_send.at[m], w_recv.at[m, 1], side)
@@ -593,10 +589,12 @@
             def _():
                 gather_second(2)
 
-        def hook_b():
-            @pl.when(k == 0)
+            @pl.when(k == 1)
             def _():
                 gather_second(3)
+
+        def hook_b():
+            pass
 
         compute_chunk(k, U, C, W, WO, TAPS, TF, TB, UT, HID, GP, PART, PSH, PFIL, ROWS, hook_a, hook_b)
         z_start(k)
@@ -629,13 +627,12 @@
     zh_start(0)
     xy_start(3)
     small_y()
-    for o, (ref, hbm) in enumerate(((out_ref, out_hbm), (grad_ref, grad_hbm))):
+    for o, ref in enumerate((out_ref, grad_ref)):
         for s in range(2):
             op[2 * o + s].wait_recv()
             rows = pl.ds(pl.multiple_of(256 * s + 128 * c, 128), 128)
             value = (OUTP[o, rows, :] + RP[o, s]).astype(BF16)
             ref[s] = value if s == 0 else mm(value, FLIP[...]).astype(BF16)
-        leave(o, ref, hbm)
     zh_start(1)
     xg_start(0)
     small_h()
@@ -650,13 +647,10 @@
     for m in range(4):
         gather_sent(m)
     small_last()
-    leave(4, gshort_ref, gshort_hbm)
-    leave(5, gfil_ref, gfil_hbm)
     for k in range(4):
         reduced(k)
     for k in range(4):
         gout_ref[pl.ds(16 * k, 16), :] = GO[k].astype(F32) * scale
-    leave(3, gout_ref, gout_hbm)
     rows = []
     for cc in range(2):
         for s in range(3):
@@ -668,26 +662,18 @@
             first, second = halves(back[32 * s:32 * s + 32, lanes], back[96 + 32 * s:128 + 32 * s, lanes])
             gin_ref[:, pl.ds(s * 1024 + t * 256, 128)] = first
             gin_ref[:, pl.ds(s * 1024 + t * 256 + 128, 128)] = second
-    leave(2, gin_ref, gin_hbm)
     for k in range(4):
         reduce_sent(k)
     small_sent()
-    for copy in departures:
-        copy.wait()
 
 
 def hand_over(*refs):
     n = 6
-    sources, targets, held = refs[:n], refs[n:2 * n], refs[2 * n:3 * n]
-    in_sem, out_sem = refs[3 * n:]
-    arrive = [pltpu.make_async_copy(sources[i], held[i], in_sem.at[i]) for i in range(n)]
-    leave = [pltpu.make_async_copy(held[i], targets[i], out_sem.at[i]) for i in range(n)]
-    for copy in arrive:
+    sems = refs[2 * n]
+    copies = [pltpu.make_async_copy(refs[i], refs[n + i], sems.at[i]) for i in range(n)]
+    for copy in copies:
         copy.start()
-    for i in range(n):
-        arrive[i].wait()
-        leave[i].start()
-    for copy in leave:
+    for copy in copies:
         copy.wait()
 
 
@@ -711,7 +697,6 @@
         pltpu.VMEM((4, 3072), F32),
         pltpu.VMEM((64, 128), BF16),
     ]
-    scratch += [pltpu.VMEM(o.shape, o.dtype) for o in outs]
     scratch += [
         pltpu.VMEM((2, 544, 512), BF16),
         pltpu.VMEM((2, 400, 512), BF16),
@@ -748,30 +733,30 @@
         pltpu.VMEM((2, 4, 16, 128), F32),
     ]
     scratch += [
-        dma((6,)), dma((6,)), dma((4,)), dma((4,)), dma((6,)), dma((6,)), dma((3,)), dma((3,)),
-        dma((4,)), dma((4, 2)), dma((4,)), dma((4, 2)),
+        dma((6,)), dma((4,)), dma((4,)), dma((6,)), dma((6,)), dma((3,)), dma((3,)),
+        dma((4,)), dma((4, 3)), dma((4,)), dma((4, 3)),
         dma((4,)), dma((4, 2)), dma((4,)), dma((4,)), dma((4,)), dma((4,)), dma((4,)), dma((4,)), dma((4,)), dma((4,)),
         dma((4,)), dma((4,)), dma((2, 2)), dma((2, 2)),
     ]
     anywhere = pl.BlockSpec(memory_space=pl.ANY)
     results = pl.pallas_call(
         functools.partial(kernel, scale),
-        out_shape=outs,
-        in_specs=[anywhere] * 6,
-        out_specs=tuple([anywhere] * 6),
+        out_shape=tuple(pltpu.VMEM(o.shape, o.dtype) for o in outs),
+        in_specs=[pl.BlockSpec(memory_space=pltpu.HBM)] * 6,
+        out_specs=tuple([pl.BlockSpec(memory_space=pltpu.VMEM)] * 6),
         scratch_shapes=scratch,
         compiler_params=pltpu.CompilerParams(
-            collective_id=0, has_side_effects=True, vmem_limit_bytes=58 * 2**20
+            collective_id=0, has_side_effects=True, vmem_limit_bytes=56 * 2**20
         ),
         cost_estimate=pl.CostEstimate(flops=9 * 10**9, bytes_accessed=4 * 10**6, transcendentals=0),
     )(strands, cotangent, proj_in, proj_out, short_taps.T, filters)
     results = pl.pallas_call(
         hand_over,
         out_shape=outs,
-        in_specs=[anywhere] * 6,
+        in_specs=[pl.BlockSpec(memory_space=pltpu.VMEM)] * 6,
         out_specs=tuple([anywhere] * 6),
-        scratch_shapes=[pltpu.VMEM(o.shape, o.dtype) for o in outs] + [dma((6,)), dma((6,))],
-    )(*results)
+        scratch_shapes=[dma((6,))],
+    )(*[pltpu.with_memory_space_constraint(r, pltpu.VMEM) for r in results])
     return results[:4] + (results[4].T, results[5])
 
 

time: 68 us -> 65.4 us (0.962)
  Pallas kernels: 67.2 us -> 64.7 us
    pallas_call x2, Pallas kernels: 67.2 us -> 64.7 us  [the longest x1 63.6 us: shards(): pl.pallas_call(functools.partial(kernel, scale), out_shape=tuple((pltpu.V...]
where the time goes in v4:
time: 65.4 us; the launch traced here: 65.3 us
  Pallas kernels  64.7 us (99%)
    pallas_call x1, Pallas kernels, shards(): pl.pallas_call(functools.partial(kernel, scale), out_shape=tuple((pltpu.V...  63.6 us

profile of v4, /device:TPU:1, one launch (start us, length us, event | category | flops | bytes accessed | tf_op | source)
XLA Modules:
  0.0 65.3 jit_solution(4379075597605368430)
XLA Ops:
  0.6 63.6 %shard_map.109 = (bf16[2,128,512]{2,1,0:T(8,128)(2,1)S(1)}, bf16[2,128,512]{2,1,0:T(8,128)(2,1)S(1)}, f32[32,3072]{1,0:T(8,128)S(1)}, f32[64,512]{1,0:T(8,128)S(...) custom-call(bf16[2,128,512]{2,1,0:T(8,128)(2,1)} %strands_hbm.1, bf16[2,128,512]{2,1,0:T(8,128)(2,1)} %cotangent_hbm.1, ...), custom_call_target="tpu_custom_call" | custom-call | flops 8999999488 | bytes 4000000 | tf_op jit(solution)/shard_map/pallas_call | solution.py:742
  64.3 1.0 %shard_map.110 = (bf16[2,128,512]{2,1,0:T(8,128)(2,1)}, bf16[2,128,512]{2,1,0:T(8,128)(2,1)}, f32[32,3072]{1,0:T(8,128)}, f32[64,512]{1,0:T(8,128)}, f32[4,192]{1,0:T(4,128)}, /*index=5*/f32[4,128]{1,0:T(4,128)}) custom-call(bf16[2,128,512]{2,1,0:T(8,128)(2,1)S(1)} %get-tuple-element.18.refs_0_, bf16[2,128,512]{2,1,0:T(8,128)(2,1)S(1)} %get-tuple-element.19.refs_1_, ...), custom_call_target="tpu_custom_call" | custom-call | tf_op jit(solution)/shard_map/pallas_call | solution.py:753

commit v5 on v4

--- a/solution.py
+++ b/solution.py
@@ -647,21 +647,22 @@
     for m in range(4):
         gather_sent(m)
     small_last()
+    def projected_back(k):
+        rows = [FIN[k, cc, :, pl.ds(128 * s, 128)] for cc in range(2) for s in range(3)]
+        return mm(jnp.concatenate(rows, axis=0), QM[:, pl.ds(128 * k, 128)], NT)
+
+    back = None
     for k in range(4):
         reduced(k)
-    for k in range(4):
         gout_ref[pl.ds(16 * k, 16), :] = GO[k].astype(F32) * scale
-    rows = []
-    for cc in range(2):
-        for s in range(3):
-            rows.append(jnp.concatenate([FIN[k, cc, :, pl.ds(128 * s, 128)] for k in range(4)], axis=1))
-    back = mm(jnp.concatenate(rows, axis=0), QM[...], NT) * scale
+        term = projected_back(k)
+        back = term if back is None else back + term
     for s in range(3):
         for t in range(4):
             lanes = slice(128 * t, 128 * t + 128)
             first, second = halves(back[32 * s:32 * s + 32, lanes], back[96 + 32 * s:128 + 32 * s, lanes])
-            gin_ref[:, pl.ds(s * 1024 + t * 256, 128)] = first
-            gin_ref[:, pl.ds(s * 1024 + t * 256 + 128, 128)] = second
+            gin_ref[:, pl.ds(s * 1024 + t * 256, 128)] = first * scale
+            gin_ref[:, pl.ds(s * 1024 + t * 256 + 128, 128)] = second * scale
     for k in range(4):
         reduce_sent(k)
     small_sent()

time: 65.4 us -> 65.3 us (level)
  no operation moved by 1% of the time
where the time goes in v5:
time: 65.3 us; the launch traced here: 65.2 us
  Pallas kernels  64.5 us (99%)
    pallas_call x1, Pallas kernels, shards(): pl.pallas_call(functools.partial(kernel, scale), out_shape=tuple((pltpu.V...  63.5 us

profile of v5, /device:TPU:1, one launch (start us, length us, event | category | flops | bytes accessed | tf_op | source)
XLA Modules:
  0.0 65.2 jit_solution(18442924539211603776)
XLA Ops:
  0.6 63.5 %shard_map.109 = (bf16[2,128,512]{2,1,0:T(8,128)(2,1)S(1)}, bf16[2,128,512]{2,1,0:T(8,128)(2,1)S(1)}, f32[32,3072]{1,0:T(8,128)S(1)}, f32[64,512]{1,0:T(8,128)S(...) custom-call(bf16[2,128,512]{2,1,0:T(8,128)(2,1)} %strands_hbm.1, bf16[2,128,512]{2,1,0:T(8,128)(2,1)} %cotangent_hbm.1, ...), custom_call_target="tpu_custom_call" | custom-call | flops 8999999488 | bytes 4000000 | tf_op jit(solution)/shard_map/pallas_call | solution.py:743
  64.1 1.0 %shard_map.110 = (bf16[2,128,512]{2,1,0:T(8,128)(2,1)}, bf16[2,128,512]{2,1,0:T(8,128)(2,1)}, f32[32,3072]{1,0:T(8,128)}, f32[64,512]{1,0:T(8,128)}, f32[4,192]{1,0:T(4,128)}, /*index=5*/f32[4,128]{1,0:T(4,128)}) custom-call(bf16[2,128,512]{2,1,0:T(8,128)(2,1)S(1)} %get-tuple-element.18.refs_0_, bf16[2,128,512]{2,1,0:T(8,128)(2,1)S(1)} %get-tuple-element.19.refs_1_, ...), custom_call_target="tpu_custom_call" | custom-call | tf_op jit(solution)/shard_map/pallas_call | solution.py:754
